TPU v7x, 32 devices: a whole 2x2x4 slice. The times are simulated.
32 devices in a mesh: dp: 4 (over y, x), seq: 2 (over core), tensor: 4 (over z).
Axes of the slice: x: 2, y: 2, z: 4, core: 2. Of those that a mesh axis runs over, the one named last changes fastest.
Arguments:
- features: bfloat16 [1024, 4096], P(('dp', 'seq'), 'tensor'), parts along dimension 0, may hold values from -6 to 6
- in_weight: bfloat16 [4096, 3, 4096], P('seq', None, 'tensor'), may hold values from -0.09375 to 0.09375
- short_taps: float32 [3, 7, 4096], P(None, None, 'tensor'), may hold values from -2.5 to 2.5
- decay_rates: float32 [16, 4096], P(None, 'tensor'), may hold values from 0.001953125 to 0.1
- residues: float32 [16, 4096], P(None, 'tensor'), may hold values from -1.5 to 1.5
- skip_gain: float32 [4096], P('tensor'), may hold values from 0.5 to 1.5
- out_weight: bfloat16 [4096, 4096], P(None, 'tensor'), may hold values from -0.09375 to 0.09375
Outputs:
- mixed: bfloat16 [1024, 4096], P(('dp', 'seq'), 'tensor'), parts along dimension 0
There are 4 independent parts, one for each index of `dp`. A program takes and returns all parts, laid end to end along the dimension named above; an argument that names none is the same for every part. Nothing has to cross between parts.
All inputs are finite; a program needn't handle non-finite values.
Results may differ from a plain program's by a relative error of at most 0.007.
Values may be sent and summed in bfloat16 or wider, within the bound.
A program may use at most 128 MiB of HBM per device.

v0:
```python
import jax
import jax.numpy as jnp
from jax import lax
from jax.sharding import PartitionSpec as P

precise = lax.Precision.HIGHEST
block_len = 64


def passed_along(value, axis, steps):
    count = lax.axis_size(axis)
    leading, last = (max(0, -steps), min(count, count - steps))
    return lax.ppermute(value, axis, [(source, source + steps) for source in range(leading, last)])


def prefix_2(part, axis, combine, identity):
    place = lax.axis_index(axis)
    gathered = jax.tree.map(lambda a: lax.all_gather(a, axis), part)
    state = jax.tree.map(lambda a, e: jnp.zeros_like(a) + jnp.asarray(e, a.dtype), part, identity)

    def one(turn, state):
        return combine(
            state, jax.tree.map(lambda a: lax.dynamic_index_in_dim(a, turn, 0, False), gathered)
        )

    return lax.fori_loop(0, place, one, state)


def body(features, in_weight, short_taps, decay_rates, residues, skip_gain, out_weight):
    tok_rows = features.shape[0]
    channels = in_weight.shape[2]
    taps_count = short_taps.shape[1]
    whole_feats = lax.all_gather(features, "tensor", axis=1, tiled=True)
    piece = lax.all_gather(in_weight, "seq", axis=0, tiled=True)
    count = piece.shape[0]
    projected = jnp.dot(
        whole_feats, piece.reshape(count, 3 * channels), preferred_element_type=jnp.float32
    )
    projected = projected.astype(jnp.bfloat16).reshape(tok_rows, 3, channels)
    rim_rows = taps_count - 1
    earlier = passed_along(projected[tok_rows - rim_rows :], "seq", 1)
    extended = jnp.concatenate([earlier, projected], axis=0).astype(jnp.float32)
    short = jnp.zeros((tok_rows, 3, channels), jnp.float32)
    for offset_lag in range(taps_count):
        short = (
            short
            + short_taps[:, offset_lag, :][None]
            * extended[rim_rows - offset_lag : rim_rows - offset_lag + tok_rows]
        )
    product = short[:, 1, :] * short[:, 2, :]
    blocks = tok_rows // block_len
    pieces = product.reshape(blocks, block_len, channels)
    amplitude = residues * jnp.sqrt(2.0 * decay_rates)
    offsets = jnp.arange(block_len).astype(jnp.float32)
    falloff = jnp.exp(-decay_rates[:, None, :] * offsets[None, :, None])
    kernel = jnp.einsum("mc,mtc->tc", amplitude, falloff, precision=precise)
    lag_grid = jnp.arange(block_len)[:, None] - jnp.arange(block_len)[None, :]
    select = (lag_grid[:, :, None] == jnp.arange(block_len)[None, None, :]).astype(jnp.float32)
    toeplitz = jnp.einsum("tsk,kc->tsc", select, kernel, precision=precise)
    inner = jnp.einsum("tsc,bsc->btc", toeplitz, pieces, precision=precise)
    toward_end = jnp.exp(-decay_rates[:, None, :] * (block_len - offsets)[None, :, None])
    block_sums = jnp.einsum("msc,bsc->bmc", toward_end, pieces, precision=precise)
    block_index = jnp.arange(blocks).astype(jnp.float32)
    carry_over = jnp.exp(
        -decay_rates[None] * (block_len * (blocks - 1 - block_index))[:, None, None]
    )
    device_sum = jnp.sum(carry_over * block_sums, axis=0)
    device_decay = jnp.exp(-decay_rates * float(tok_rows))

    def combine(earlier_pair, later_pair):
        return (earlier_pair[0] * later_pair[0], later_pair[0] * earlier_pair[1] + later_pair[1])

    prefix = prefix_2(
        (device_decay, device_sum),
        "seq",
        combine,
        (jnp.ones_like(device_decay), jnp.zeros_like(device_sum)),
    )
    entering = prefix[1]
    step_decay = jnp.exp(-decay_rates * float(block_len))

    def advance(state, block_sum):
        return (step_decay * state + block_sum, state)

    final_state, starts = lax.scan(advance, entering, block_sums)
    outer = jnp.einsum("mic,bmc->bic", amplitude[:, None, :] * falloff, starts, precision=precise)
    conv = (inner + outer).reshape(tok_rows, channels)
    gated = (short[:, 0, :] * (conv + skip_gain[None, :] * product)).astype(jnp.bfloat16)
    mixed = jnp.dot(
        lax.all_gather(gated, "tensor", axis=1, tiled=True),
        out_weight,
        preferred_element_type=jnp.float32,
    )
    return mixed.astype(jnp.bfloat16)


def solution(mesh):
    in_specs = (
        P(("dp", "seq"), "tensor"),
        P("seq", None, "tensor"),
        P(None, None, "tensor"),
        P(None, "tensor"),
        P(None, "tensor"),
        P("tensor"),
        P(None, "tensor"),
    )
    out_specs = P(("dp", "seq"), "tensor")
    return jax.shard_map(body, mesh=mesh, in_specs=in_specs, out_specs=out_specs, check_vma=False)
```

profile of v0, /device:TPU:1, one launch (start us, length us, event | category | flops | bytes accessed | tf_op | source)
XLA Modules:
  0.0 276.1 jit_solution(4304894095701675961)
XLA Ops:
  6.5 0.0 all-gather.6.cloned.1.call-start
  6.5 0.7 all-gather.6.cloned.1.call-update
  7.3 0.0 all-gather.8.cloned.1.call-start
  7.3 17.0 %copy.61 = bf16[2048,3,1024]{0,2,1:T(8,128)(2,1)} copy(bf16[2048,3,1024]{2,0,1:T(8,128)(2,1)} %param.12) | data formatting | bytes 25165824 | tf_op args[1]
  24.3 0.0 copy-start.4
  24.3 0.0 copy-start.5
  24.3 0.0 copy-start.3
  24.3 0.0 all-gather.8.cloned.1.call-update
  24.3 0.0 all-gather.10.cloned.1.call-start
  24.4 0.8 copy-done.4
  25.1 0.0 copy-done.5
  25.2 0.2 copy.92
  25.4 0.2 copy.66
  25.6 0.0 copy-start.1
  25.7 0.0 copy-done.3
  25.7 0.1 fusion.31
  25.8 11.8 %multiply_reduce_fusion = f32[1024,64]{1,0:T(8,128)S(1)} fusion(f32[1024,16]{1,0:T(8,128)S(1)} %copy.92, f32[64]{0:T(128)S(1)} %iota_convert_fusion, f32[16,1024]{0,1:T(8,128)S(1)} %copy.66), kind=kLoop, calls=%fused_computation.4 | loop fusion | flops 3080192 | bytes 393472
  37.6 11.4 %fusion.10 = f32[64,64,1024]{2,1,0:T(8,128)} fusion(s32[64,64]{1,0:T(8,128)S(1)} %iota_subtract_fusion, f32[1024,64]{1,0:T(8,128)S(1)} %multiply_reduce_fusion), kind=kOutput, calls=%fused_computation.18 | convolution fusion | flops 3221487616 | bytes 17055744 | tf_op jit(solution)/shard_map/tsk,kc->tsc/dot_general | solution.py:59
  49.0 0.0 copy-done.1
  49.0 0.0 all-gather.6.cloned.1.call-done
  49.0 31.8 %all-gather.8.cloned.1.call-done = bf16[4096,3,1024]{0,2,1:T(8,128)(2,1)} async-done(((bf16[2048,3,1024]{0,2,1:T(8,128)(2,1)}), bf16[4096,3,1024]{0,2,1:T(8,128)(2,1)}) %all-gather.8.cloned.1.call-update) | async-done | bytes 25165840 | tf_op jit(solution)/shard_map/all_gather | solution.py:34
  80.7 13.3 %convolution_convert_fusion = bf16[128,3072]{1,0:T(8,128)(2,1)S(1)} fusion(bf16[128,4096]{1,0:T(8,128)(2,1)} %all-gather.6.cloned.1.call-done, bf16[4096,3072]{0,1:T(8,128)(2,1)} %bitcast.70), kind=kOutput, calls=%fused_computation.16 | convolution fusion | flops 3221618688 | bytes 27000832 | tf_op jit(solution)/shard_map/dot_general | solution.py:36
  94.1 1.3 collective-permute-start
  95.4 1.0 copy.73
  96.4 30.5 %copy.68 = f32[64,64,1024]{1,0,2:T(8,128)} copy(f32[64,64,1024]{2,1,0:T(8,128)} %fusion.10) | data formatting | bytes 33554432 | tf_op jit(solution)/shard_map/tsk,kc->tsc/dot_general | solution.py:59
  126.9 2.7 all-gather
  129.6 0.4 copy.63
  129.9 0.0 collective-permute-done
  129.9 0.4 copy.64
  130.4 0.6 maximum_convert_fusion
  131.0 6.1 %fusion.11 = f32[128,3,1024]{0,2,1:T(8,128)S(1)} fusion(f32[134,3,1024]{0,2,1:T(8,128)S(1)} %maximum_convert_fusion, f32[3,1024]{1,0:T(4,128)S(1)} %get-tuple-element.141, f32[3,1024]{1,0:T(4,128)S(1)} %get-tuple-element.142, f32[3,1024]{1,0:T(4,128)S(1)} %get-tuple-element.143, f32[3,1024]{1,0:T(4,128)S(1)} %get-tuple-element.144, ...), kind=kLoop, calls=%fused_computation.20 | loop fusion | flops 5111808 | bytes 12668928 | tf_op jit(solution)/shard_map/add | solution.py:46
  137.0 0.1 slice_multiply_fusion.7
  137.1 0.2 copy.65
  137.3 0.6 copy.67
  137.9 0.0 copy-start.2
  137.9 56.5 %fusion.32 = f32[1024,2,64]{2,1,0:T(2,128)} fusion(f32[2,64,1024]{1,0,2:T(2,128)S(1)} %copy.67, f32[64,64,1024]{1,0,2:T(8,128)} %copy.68), kind=kOutput, calls=%fused_computation.61 | convolution fusion | flops 100663296 | bytes 17825792 | tf_op jit(solution)/shard_map/tsc,bsc->btc/dot_general | solution.py:60
  194.4 0.0 copy-done.2
  194.4 18.8 %multiply_reduce_fusion.1 = (f32[16,1024]{0,1:T(8,128)}, f32[2,16,1024]{1,0,2:T(2,128)}) fusion(f32[16,1024]{0,1:T(8,128)S(1)} %copy-done.2, f32[2]{0:T(128)S(1)} %subtract_multiply_fusion, f32[2,64,1024]{1,0,2:T(2,128)S(1)} %copy.67, f32[64]{0:T(128)S(1)} %broadcast_subtract_fusion), kind=kOutput, calls=%fused_computation.37 | convolution fusion | flops 26296320 | bytes 786696 | tf_op jit(solution)/shard_map/msc,bsc->bmc/dot_general | solution.py:62
  213.1 1.2 copy.71
  214.3 0.0 copy-start
  214.3 2.0 all-gather.1
  216.4 1.6 copy.72
  218.1 0.1 while.25
  218.2 1.2 copy.74
  219.4 0.0 copy-done
  219.4 0.0 copy-start.6
  219.5 12.9 %fusion.20 = f32[2,64,1024]{1,0,2:T(2,128)} fusion(f32[1024,2,64]{2,1,0:T(2,128)S(1)} %copy-done, f32[2,16,1024]{1,0,2:T(2,128)} %copy.74, f32[16,1024]{0,1:T(8,128)} %copy.73, f32[64]{0:T(128)S(1)} %iota_convert_fusion, f32[16,1024]{0,1:T(8,128)} %copy-done.1), kind=kOutput, calls=%fused_computation.34 | convolution fusion | flops 27394048 | bytes 1310976 | tf_op jit(solution)/shard_map/mic,bmc->bic/dot_general | solution.py:86
  232.4 1.4 copy.75
  233.8 0.2 copy.76
  234.0 0.0 copy-done.6
  234.0 0.9 fusion.28
  234.9 0.0 all-gather.10.cloned.1.call-update
  235.0 28.8 %all-gather.10.cloned.1.call-done = bf16[128,4096]{0,1:T(8,128)(2,1)} async-done(((bf16[128,1024]{0,1:T(8,128)(2,1)}), bf16[128,4096]{0,1:T(8,128)(2,1)}) %all-gather.10.cloned.1.call-update) | async-done | bytes 1048592 | tf_op jit(solution)/shard_map/all_gather | solution.py:90
  263.8 5.7 %convolution_convert_fusion.1 = bf16[128,1024]{1,0:T(8,128)(2,1)} fusion(bf16[128,4096]{0,1:T(8,128)(2,1)} %all-gather.10.cloned.1.call-done, bf16[4096,1024]{1,0:T(8,128)(2,1)} %param.17), kind=kOutput, calls=%fused_computation.36 | convolution fusion | flops 1073872896 | bytes 9699328 | tf_op jit(solution)/shard_map/dot_general | solution.py:89
  (18 shorter events, 0.2 us)
Async XLA Ops:
  6.5 42.4 %all-gather.6.cloned.1.call-start = ((), (), s32[]{:S(2)}) async-start(), calls=%async_computation | async-start | bytes 1310720 | tf_op jit(solution)/shard_map/all_gather | solution.py:33
  7.3 73.5 %all-gather.8.cloned.1.call-start = ((), (), s32[]{:S(2)}) async-start(), calls=%async_computation.1 | async-start | bytes 37748736 | tf_op jit(solution)/shard_map/all_gather | solution.py:34
  24.3 0.8 copy-start.4
  24.3 0.9 copy-start.5
  24.3 1.4 copy-start.3
  24.3 239.5 %all-gather.10.cloned.1.call-start = ((), (), s32[]{:S(2)}) async-start(), calls=%async_computation.2 | async-start | bytes 1310720 | tf_op jit(solution)/shard_map/all_gather | solution.py:90
  25.6 23.4 %copy-start.1 = (f32[16,1024]{0,1:T(8,128)}, f32[16,1024]{0,1:T(8,128)S(1)}, u32[]{:S(2)}) copy-start(f32[16,1024]{0,1:T(8,128)S(1)} %copy.66) | copy-start | bytes 196612
  94.1 35.8 %collective-permute-start = (bf16[6,3,1024]{2,0,1:T(8,128)(2,1)S(1)}, bf16[6,3,1024]{2,0,1:T(8,128)(2,1)S(1)}, u32[]{:S(2)}, u32[]{:S(2)}) collective-permute-start(bf16[6,3,1024]{2,0,1:T(8,128)(2,1)S(1)} %bitcast.78), channel_id=1, source_target_pairs={{0,4},{1,5},{2,6},{3,7},{8,12},{9,13},{10,14},{11,15},{16,20},{17,... | collective-permute-start | bytes 110600 | tf_op jit(solution)/shard_map/ppermute | solution.py:13
  137.9 56.5 %copy-start.2 = (f32[16,1024]{0,1:T(8,128)S(1)}, f32[16,1024]{0,1:T(8,128)}, u32[]{:S(2)}) copy-start(f32[16,1024]{0,1:T(8,128)} %copy-done.1) | copy-start | bytes 196612
  214.3 5.1 %copy-start = (f32[1024,2,64]{2,1,0:T(2,128)S(1)}, f32[1024,2,64]{2,1,0:T(2,128)}, u32[]{:S(2)}) copy-start(f32[1024,2,64]{2,1,0:T(2,128)} %fusion.32) | copy-start | bytes 1572868
  219.4 14.6 %copy-start.6 = (f32[1024]{0:T(1024)S(1)}, f32[1024]{0:T(1024)}, u32[]{:S(2)}) copy-start(f32[1024]{0:T(1024)} %param.16) | copy-start | bytes 12292
Sparse Core Ops, SparseCore 0:
  8.9 29.8 all-gather.5
  40.4 40.2 all-gather.7
  235.1 28.6 all-gather.9
where the time goes:
time: 278 us; the launch traced here: 276 us
  matrix products  119 us (43%)
  waiting for transfers between devices  61.3 us (22%)
  local copies, waits for them, and re-layouts  57 us (21%)
  other arithmetic  19.5 us (7%)
  between operations  13.4 us (5%)
  blocking collectives  4.69 us (2%)
    dot_general x1, matrix products, body(): inner = jnp.einsum('tsc,bsc->btc', toeplitz, pieces, precision=precise)  56.5 us
    all_gather x1, waiting for transfers between devices, body(): piece = lax.all_gather(in_weight, 'seq', axis=0, tiled=True)  31.8 us
    dot_general x1, local copies, waits for them, and re-layouts, body(): toeplitz = jnp.einsum('tsk,kc->tsc', select, kernel, precision=precise)  30.5 us
    all_gather x1, waiting for transfers between devices, body(): lax.all_gather(gated, 'tensor', axis=1, tiled=True)  28.8 us
    dot_general x1, matrix products, body(): jnp.einsum('msc,bsc->bmc', toward_end, pieces, precision=precise)  18.8 us
    unnamed x20, local copies, waits for them, and re-layouts  18 us
    dot_general x1, matrix products, body(): jnp.dot(whole_feats, piece.reshape(count, 3 * channels), preferred_elemen...  13.3 us
    dot_general x1, matrix products, body(): jnp.einsum('mic,bmc->bic', amplitude[:, None, :] * falloff, starts, preci...  12.9 us
  transfers between devices with their start and end apart: 4, of which 2 were waited for; matrix products, arithmetic and copies ran while one was open for 26% of the time, Pallas kernels for 0%

commit v1 on v0

--- a/solution.py
+++ b/solution.py
@@ -1,7 +1,13 @@
+import functools
+
 import jax
 import jax.numpy as jnp
 from jax import lax
+from jax.experimental import pallas as pl
+from jax.experimental.pallas import tpu as pltpu
 from jax.sharding import PartitionSpec as P
+
+MESH = pl.DeviceIdType.MESH
 
 precise = lax.Precision.HIGHEST
 block_len = 64
@@ -94,6 +100,310 @@
     return mixed.astype(jnp.bfloat16)
 
 
+def nearest_first(place, step):
+    table = ((0, 1, 2, 3), (1, 0, 2, 3), (2, 3, 1, 0), (3, 2, 1, 0))
+    found = jnp.int32(table[0][step])
+    for at in range(1, 4):
+        found = jnp.where(place == at, jnp.int32(table[at][step]), found)
+    return found
+
+
+def fused_kernel(
+    feat, w_hbm, taps, decay, resid, skip, ow_hbm, out,
+    f, w, ow, psend, precv, own, proj, prod, gate, gbuf, gsend, gath, acc,
+    f_send, f_recv, w_sem, ow_sem, p_send, p_recv, g_send, g_recv,
+):
+    rows, deep = feat.shape
+    half = own.shape[-1] * 4
+    tile = half // 2
+    lanes = own.shape[-1]
+    span = 2 * rows // 8
+    modes = decay.shape[0]
+    taps_count = taps.shape[1]
+    rim = taps_count - 1
+    s = lax.axis_index("seq")
+    t = lax.axis_index("tensor")
+    me = t * 2 + s
+    others = [(ds, dt) for dt in range(4) for ds in range(2) if (ds, dt) != (0, 0)]
+
+    def device(ds, dt):
+        return {"seq": lax.rem(s + ds, 2), "tensor": lax.rem(t + dt, 4)}
+
+    near = jnp.where(t > 2 * s, 1, 0)
+
+    def w_copy(step, j):
+        r = near if step == 0 else 1 - near
+        rng = pl.ds(pl.multiple_of(r * deep, deep), deep)
+        return pltpu.make_async_copy(w_hbm.at[j, rng], w.at[j, rng], w_sem.at[step, j])
+
+    def ow_copy(k):
+        rng = pl.ds(k * deep, deep)
+        return pltpu.make_async_copy(ow_hbm.at[rng], ow.at[rng], ow_sem.at[k])
+
+    for step in range(2):
+        for j in range(3):
+            w_copy(step, j).start()
+
+    barrier = pltpu.get_barrier_semaphore()
+    for ds, dt in others:
+        pl.semaphore_signal(barrier, inc=1, device_id=device(ds, dt), device_id_type=MESH)
+    pl.semaphore_wait(barrier, len(others))
+
+    home = t // 2
+    slot = lax.rem(t, 2)
+    place = pl.ds(pl.multiple_of(s * rows, rows), rows)
+
+    def f_push(dt):
+        return pltpu.make_async_remote_copy(
+            src_ref=feat,
+            dst_ref=f.at[slot, place],
+            send_sem=f_send.at[dt],
+            recv_sem=f_recv.at[slot, s],
+            device_id={"seq": home, "tensor": lax.rem(t + dt, 4)},
+            device_id_type=MESH,
+        )
+
+    def f_own():
+        return pltpu.make_async_copy(feat, f.at[slot, place], f_recv.at[slot, s])
+
+    for dt in (2, 3, 1):
+        f_push(dt).start()
+
+    @pl.when(home == s)
+    def _():
+        f_own().start()
+
+    @pl.when(home != s)
+    def _():
+        f_push(0).start()
+
+    for k in range(4):
+        ow_copy(k).start()
+
+    def p_push(ct, j):
+        return pltpu.make_async_remote_copy(
+            src_ref=psend.at[ct, j],
+            dst_ref=precv.at[ct, j],
+            send_sem=p_send.at[ct, j],
+            recv_sem=p_recv.at[ct, j],
+            device_id=device(1, 0),
+            device_id_type=MESH,
+        )
+
+    for step in range(2):
+        r = near if step == 0 else 1 - near
+        for h in range(2):
+            part = f.at[r, pl.ds(h * rows, rows)]
+            pltpu.make_async_copy(part, part, f_recv.at[r, h]).wait()
+        for j in range(3):
+            w_copy(step, j).wait()
+        depth = pl.ds(pl.multiple_of(r * deep, deep), deep)
+        for side in range(2):
+            target = psend if side == 0 else own
+            base = ((1 - s) if side == 0 else s) * half
+
+            @pl.loop(0, 6)
+            def _(idx, target=target, base=base, side=side, step=step, r=r, depth=depth):
+                ct, j = idx // 3, lax.rem(idx, 3)
+                columns = pl.ds(pl.multiple_of(base + ct * tile, tile), tile)
+                part = jnp.dot(f[r], w[j, depth, columns], preferred_element_type=jnp.float32)
+                for gl in range(2):
+                    piece = part[:, gl * lanes : (gl + 1) * lanes]
+                    if step == 0:
+                        target[ct, j, gl] = piece
+                    else:
+                        target[ct, j, gl] += piece
+                if step == 1 and side == 0:
+                    p_push(ct, j).start()
+
+    first = lax.broadcasted_iota(jnp.int32, (8, lanes), 0)
+
+    def later(value, by):
+        return jnp.where(first >= by, pltpu.roll(value, by, 0), 0.0)
+
+    def g_push(n, ct):
+        ds, dt = others[n]
+        to = lax.rem(s + ds, 2)
+        return pltpu.make_async_remote_copy(
+            src_ref=gsend.at[ct, pl.ds(pl.multiple_of(to * rows, rows), rows)],
+            dst_ref=gath.at[me, :, pl.ds(pl.multiple_of(ct * tile, tile), tile)],
+            send_sem=g_send.at[n, ct],
+            recv_sem=g_recv.at[me, ct],
+            device_id=device(ds, dt),
+            device_id_type=MESH,
+        )
+
+    @pl.loop(0, 2)
+    def _(ct):
+        for j in range(3):
+            part = precv.at[ct, j]
+            pltpu.make_async_copy(part, part, p_recv.at[ct, j]).wait()
+
+        for gl in range(2):
+            columns = pl.ds(pl.multiple_of(s * half + ct * tile + gl * lanes, lanes), lanes)
+
+            @pl.loop(0, span)
+            def _(i, gl=gl):
+                at = pl.ds(i, 8, stride=span)
+                for j in range(3):
+                    value = own.at[ct, j, gl][at, :] + precv.at[ct, j, gl][at, :]
+                    proj[j, rim + i] = value.astype(jnp.bfloat16).astype(jnp.float32)
+
+            for j in range(3):
+                for k in range(rim):
+                    proj[j, k] = later(proj[j, span + k], 1)
+
+            tap = [
+                [jnp.broadcast_to(taps[j, k : k + 1, columns], (8, lanes)) for k in range(taps_count)]
+                for j in range(3)
+            ]
+            rate = [jnp.broadcast_to(decay[m : m + 1, columns], (8, lanes)) for m in range(modes)]
+
+            @pl.loop(0, span, unroll=2)
+            def _(i, tap=tap):
+                short = []
+                for j in range(3):
+                    total = tap[j][0] * proj[j, rim + i]
+                    for k in range(1, taps_count):
+                        total = total + tap[j][k] * proj[j, rim + i - k]
+                    short.append(total)
+                gate[i] = short[0]
+                prod[i] = short[1] * short[2]
+
+            fall = [jnp.exp(-v) for v in rate]
+
+            def gather_state(i, state, fall=fall):
+                x = prod[i]
+                return tuple(a * v + x for a, v in zip(fall, state))
+
+            zero = jnp.zeros((8, lanes), jnp.float32)
+            state = lax.fori_loop(0, span, gather_state, (zero,) * modes, unroll=4)
+            start = []
+            for m in range(modes):
+                jump = jnp.exp(-rate[m] * float(span))
+                value = later(state[m], 1)
+                for by in (1, 2, 4):
+                    value = value + jump * later(value, by)
+                    jump = jump * jump
+                start.append(value)
+            scale = [
+                jnp.broadcast_to(resid[m : m + 1, columns], (8, lanes)) * jnp.sqrt(2.0 * rate[m])
+                for m in range(modes)
+            ]
+            direct = jnp.broadcast_to(skip[:, columns], (8, lanes))
+
+            def emit(i, state, fall=fall, scale=scale, direct=direct):
+                x = prod[i]
+                state = tuple(a * v + x for a, v in zip(fall, state))
+                terms = [a * v for a, v in zip(scale, state)]
+                while len(terms) > 1:
+                    terms = [a + b for a, b in zip(terms[::2], terms[1::2])]
+                gbuf[pl.ds(i, 8, stride=span), :] = gate[i] * (terms[0] + direct * x)
+                return state
+
+            lax.fori_loop(0, span, emit, tuple(start), unroll=2)
+            gsend[ct, :, gl * lanes : (gl + 1) * lanes] = gbuf[...].astype(jnp.bfloat16)
+
+        for n in range(len(others)):
+            g_push(n, ct).start()
+        gath[me, :, pl.ds(pl.multiple_of(ct * tile, tile), tile)] = gsend[
+            ct, pl.ds(pl.multiple_of(s * rows, rows), rows)
+        ]
+
+    for k in range(4):
+        ow_copy(k).wait()
+
+    for step in range(4):
+        z = nearest_first(t, step)
+        for ds in range(2):
+            source = z * 2 + lax.rem(s + ds, 2)
+            if (step, ds) != (0, 0):
+                for ct in range(2):
+                    part = gath.at[source, :, pl.ds(ct * tile, tile)]
+                    pltpu.make_async_copy(part, part, g_recv.at[source, ct]).wait()
+            depth = pl.ds(pl.multiple_of(source * half, half), half)
+            part = jnp.dot(gath[source], ow[depth, :], preferred_element_type=jnp.float32)
+            if (step, ds) == (0, 0):
+                acc[...] = part
+            elif (step, ds) == (3, 1):
+                out[...] = (acc[...] + part).astype(out.dtype)
+            else:
+                acc[...] += part
+
+    for dt in (1, 2, 3):
+        f_push(dt).wait_send()
+
+    @pl.when(home != s)
+    def _():
+        f_push(0).wait_send()
+
+    for ct in range(2):
+        for j in range(3):
+            p_push(ct, j).wait_send()
+        for n in range(len(others)):
+            g_push(n, ct).wait_send()
+
+
+def fused_body(features, in_weight, short_taps, decay_rates, residues, skip_gain, out_weight):
+    rows, deep = features.shape
+    channels = in_weight.shape[2]
+    half = channels // 2
+    tile = half // 2
+    lanes = tile // 2
+    span = 2 * rows // 8
+    rim = short_taps.shape[1] - 1
+    f32, bf16 = jnp.float32, jnp.bfloat16
+    dma = pltpu.SemaphoreType.DMA
+    vmem = pl.BlockSpec(memory_space=pltpu.VMEM)
+    hbm = pl.BlockSpec(memory_space=pl.ANY)
+    return pl.pallas_call(
+        fused_kernel,
+        out_shape=jax.ShapeDtypeStruct((rows, channels), bf16),
+        in_specs=[hbm, hbm, vmem, vmem, vmem, vmem, hbm],
+        out_specs=vmem,
+        scratch_shapes=[
+            pltpu.VMEM((2, 2 * rows, deep), bf16),
+            pltpu.VMEM((3, 2 * deep, channels), bf16),
+            pltpu.VMEM((4 * channels, channels), bf16),
+            pltpu.VMEM((2, 3, 2, 2 * rows, lanes), f32),
+            pltpu.VMEM((2, 3, 2, 2 * rows, lanes), f32),
+            pltpu.VMEM((2, 3, 2, 2 * rows, lanes), f32),
+            pltpu.VMEM((3, span + rim, 8, lanes), f32),
+            pltpu.VMEM((span, 8, lanes), f32),
+            pltpu.VMEM((span, 8, lanes), f32),
+            pltpu.VMEM((2 * rows, lanes), f32),
+            pltpu.VMEM((2, 2 * rows, tile), bf16),
+            pltpu.VMEM((8, rows, half), bf16),
+            pltpu.VMEM((rows, channels), f32),
+            dma((4,)),
+            dma((2, 2)),
+            dma((2, 3)),
+            dma((4,)),
+            dma((2, 3)),
+            dma((2, 3)),
+            dma((7, 2)),
+            dma((8, 2)),
+        ],
+        compiler_params=pltpu.CompilerParams(
+            collective_id=0, has_side_effects=True, vmem_limit_bytes=50 * 1024 * 1024
+        ),
+        cost_estimate=pl.CostEstimate(
+            flops=2 * rows * 4 * channels * 4 * channels,
+            bytes_accessed=10 * deep * channels * 2,
+            transcendentals=0,
+        ),
+        name="mixer",
+    )(
+        features,
+        jnp.transpose(in_weight, (1, 0, 2)),
+        short_taps,
+        decay_rates,
+        residues,
+        skip_gain[None, :],
+        out_weight,
+    )
+
+
 def solution(mesh):
     in_specs = (
         P(("dp", "seq"), "tensor"),
@@ -105,4 +415,8 @@
         P(None, "tensor"),
     )
     out_specs = P(("dp", "seq"), "tensor")
+    if mesh.shape["seq"] == 2 and mesh.shape["tensor"] == 4:
+        return jax.shard_map(
+            fused_body, mesh=mesh, in_specs=in_specs, out_specs=out_specs, check_vma=False
+        )
     return jax.shard_map(body, mesh=mesh, in_specs=in_specs, out_specs=out_specs, check_vma=False)

time: 278 us -> 64.6 us (0.23)
  matrix products: 119 us -> 0 us
  waiting for transfers between devices: 61.3 us -> 0 us
  Pallas kernels: 0 us -> 59.3 us
  local copies, waits for them, and re-layouts: 57 us -> 4.91 us
  other arithmetic: 19.5 us -> 0 us
  between operations: 13.4 us -> 0.01 us
  blocking collectives: 4.69 us -> 0 us
    dot_general x6 -> x0, matrix products: 119 us -> none  [the longest x1 56.5 us: body(): inner = jnp.einsum('tsc,bsc->btc', toeplitz, pieces, precision=precise)]
    all_gather x3 -> x0, waiting for transfers between devices: 60.6 us -> none  [the longest x1 31.8 us: body(): piece = lax.all_gather(in_weight, 'seq', axis=0, tiled=True)]
    pallas_call x0 -> x1, Pallas kernels: none -> 59.3 us  [fused_body(): pl.pallas_call(fused_kernel, out_shape=jax.ShapeDtypeStruct((rows, channe...]
    dot_general x1 -> x0, local copies, waits for them, and re-layouts: 30.5 us -> none  [body(): toeplitz = jnp.einsum('tsk,kc->tsc', select, kernel, precision=precise)]
    unnamed x20 -> x11, local copies, waits for them, and re-layouts: 18 us -> 4.91 us
    unnamed x1 -> x0, other arithmetic: 11.8 us -> none
    add x4 -> x0, other arithmetic: 6.13 us -> none  [the longest x1 6.06 us: body(): short + short_taps[:, offset_lag, :][None] * extended[rim_rows - offset_l...]
    all_gather x2 -> x0, blocking collectives: 4.69 us -> none  [prefix_2(): gathered = jax.tree.map(lambda a: lax.all_gather(a, axis), part)]
  transfers between devices with their start and end apart: 4 -> 0, of which waited for: 2 -> 0; matrix products, arithmetic and copies ran while one was open for 26% -> 0% of each run, Pallas kernels for 0% -> 0%
where the time goes in v1:
time: 64.6 us; the launch traced here: 64.3 us
  Pallas kernels  59.3 us (92%)
  local copies, waits for them, and re-layouts  4.91 us (8%)
    pallas_call x1, Pallas kernels, fused_body(): pl.pallas_call(fused_kernel, out_shape=jax.ShapeDtypeStruct((rows, channe...  59.3 us
    unnamed x11, local copies, waits for them, and re-layouts  4.91 us

profile of v1, /device:TPU:1, one launch (start us, length us, event | category | flops | bytes accessed | tf_op | source)
XLA Modules:
  0.0 64.3 jit_solution(4215398005116885890)
XLA Ops:
  0.0 0.0 copy-start
  0.0 0.9 %copy-done = bf16[128,1024]{1,0:T(8,128)(2,1)S(1)} copy-done((bf16[128,1024]{1,0:T(8,128)(2,1)S(1)}, bf16[128,1024]{1,0:T(8,128)(2,1)}, u32[]{:S(2)}) %copy-start) | copy-done | bytes 262168
  1.0 0.0 copy-start.1
  1.0 0.9 %copy-done.1 = f32[3,7,1024]{2,1,0:T(8,128)S(1)} copy-done((f32[3,7,1024]{2,1,0:T(8,128)S(1)}, f32[3,7,1024]{2,1,0:T(8,128)}, u32[]{:S(2)}) %copy-start.1) | copy-done | bytes 86040
  1.8 0.0 copy-start.2
  1.8 0.8 %copy-done.2 = f32[16,1024]{1,0:T(8,128)S(1)} copy-done((f32[16,1024]{1,0:T(8,128)S(1)}, f32[16,1024]{1,0:T(8,128)}, u32[]{:S(2)}) %copy-start.2) | copy-done | bytes 65560
  2.7 0.0 copy-start.3
  2.7 0.8 %copy-done.3 = f32[16,1024]{1,0:T(8,128)S(1)} copy-done((f32[16,1024]{1,0:T(8,128)S(1)}, f32[16,1024]{1,0:T(8,128)}, u32[]{:S(2)}) %copy-start.3) | copy-done | bytes 65560
  3.5 0.0 copy-start.4
  3.5 0.7 %copy-done.4 = f32[1024]{0:T(1024)S(1)} copy-done((f32[1024]{0:T(1024)S(1)}, f32[1024]{0:T(1024)}, u32[]{:S(2)}) %copy-start.4) | copy-done | bytes 4120
  4.2 59.3 %mixer.1 = bf16[128,1024]{1,0:T(8,128)(2,1)S(1)} custom-call(bf16[128,1024]{1,0:T(8,128)(2,1)S(1)} %copy-done, bf16[3,2048,1024]{2,1,0:T(8,128)(2,1)} %bitcast.3, f32[3,7,1024]{2,1,0:T(8,128)S(1)} %copy-done.1, f32[16,1024]{1,0:T(8,128)S(1)} %copy-done.2, f32[16,1024]{1,0:T(8,128)S(1)} %copy-done.3, f32[1,1024]{1,0:T(1,128)S(1)} %bitcast.2, ...), custom_call_target="tpu_custom_call" | custom-call | flops 4294967296 | bytes 20971520 | tf_op jit(solution)/shard_map/mixer/pallas_call | solution.py:359
  63.6 0.7 %copy.9 = bf16[128,1024]{1,0:T(8,128)(2,1)} copy(bf16[128,1024]{1,0:T(8,128)(2,1)S(1)} %mixer.1) | data formatting | bytes 524288
Async XLA Ops:
  0.0 0.9 %copy-start = (bf16[128,1024]{1,0:T(8,128)(2,1)S(1)}, bf16[128,1024]{1,0:T(8,128)(2,1)}, u32[]{:S(2)}) copy-start(bf16[128,1024]{1,0:T(8,128)(2,1)} %feat.1) | copy-start | bytes 786436
  1.0 0.9 %copy-start.1 = (f32[3,7,1024]{2,1,0:T(8,128)S(1)}, f32[3,7,1024]{2,1,0:T(8,128)}, u32[]{:S(2)}) copy-start(f32[3,7,1024]{2,1,0:T(8,128)} %taps.1) | copy-start | bytes 258052
  1.8 0.8 %copy-start.2 = (f32[16,1024]{1,0:T(8,128)S(1)}, f32[16,1024]{1,0:T(8,128)}, u32[]{:S(2)}) copy-start(f32[16,1024]{1,0:T(8,128)} %decay.1) | copy-start | bytes 196612
  2.7 0.8 %copy-start.3 = (f32[16,1024]{1,0:T(8,128)S(1)}, f32[16,1024]{1,0:T(8,128)}, u32[]{:S(2)}) copy-start(f32[16,1024]{1,0:T(8,128)} %resid.1) | copy-start | bytes 196612
  3.5 0.7 %copy-start.4 = (f32[1024]{0:T(1024)S(1)}, f32[1024]{0:T(1024)}, u32[]{:S(2)}) copy-start(f32[1024]{0:T(1024)} %param.12) | copy-start | bytes 12292

commit v2 on v0

--- a/solution.py
+++ b/solution.py
@@ -1,7 +1,13 @@
+import functools
+
 import jax
 import jax.numpy as jnp
 from jax import lax
+from jax.experimental import pallas as pl
+from jax.experimental.pallas import tpu as pltpu
 from jax.sharding import PartitionSpec as P
+
+MESH = pl.DeviceIdType.MESH
 
 precise = lax.Precision.HIGHEST
 block_len = 64
@@ -94,6 +100,429 @@
     return mixed.astype(jnp.bfloat16)
 
 
+def arrival_order(place, step):
+    table = ((0, 1, 2, 3), (1, 3, 0, 2), (2, 0, 3, 1), (3, 2, 1, 0))
+    found = jnp.int32(table[0][step])
+    for at in range(1, 4):
+        found = jnp.where(place == at, jnp.int32(table[at][step]), found)
+    return found
+
+
+def fused_kernel(
+    feat, w_hbm, taps_hbm, decay_hbm, resid_hbm, skip_hbm, ow_hbm, out,
+    f, w, ow, taps, decay, resid, skip, psend, precv, own, proj, prod, gate, rims, carry,
+    gbuf, gsend, gath, acc,
+    f_send, f_recv, fr_send, w_sem, ow_sem, c_sem, p_send, p_recv, g_send, g_recv, gr_send,
+):
+    rows, deep = feat.shape
+    lanes = own.shape[-1]
+    half = lanes * 4
+    tile = half // 2
+    span = rows // 8
+    modes = decay.shape[0]
+    taps_count = taps.shape[1]
+    rim = taps_count - 1
+    s = lax.axis_index("seq")
+    t = lax.axis_index("tensor")
+    me = t * 2 + s
+    others = [(ds, dt) for dt in range(4) for ds in range(2) if (ds, dt) != (0, 0)]
+
+    def device(ds, dt):
+        return {"seq": lax.rem(s + ds, 2), "tensor": lax.rem(t + dt, 4)}
+
+    near = jnp.where(t > 2 * s, 1, 0)
+    mine = pl.ds(pl.multiple_of(s * half, half), half)
+
+    def w_copy(step, j):
+        r = near if step == 0 else 1 - near
+        rng = pl.ds(pl.multiple_of(r * deep, deep), deep)
+        return pltpu.make_async_copy(w_hbm.at[j, rng], w.at[j, rng], w_sem.at[step, j])
+
+    def ow_copy(k):
+        rng = pl.ds(k * deep, deep)
+        return pltpu.make_async_copy(ow_hbm.at[rng], ow.at[rng], ow_sem.at[k])
+
+    small = [
+        pltpu.make_async_copy(taps_hbm.at[:, :, mine], taps, c_sem.at[0]),
+        pltpu.make_async_copy(decay_hbm.at[:, mine], decay, c_sem.at[1]),
+        pltpu.make_async_copy(resid_hbm.at[:, mine], resid, c_sem.at[2]),
+        pltpu.make_async_copy(skip_hbm.at[:, mine], skip, c_sem.at[3]),
+    ]
+
+    barrier = pltpu.get_barrier_semaphore()
+    for ds, dt in others:
+        pl.semaphore_signal(barrier, inc=1, device_id=device(ds, dt), device_id_type=MESH)
+    for step in range(2):
+        for j in range(3):
+            w_copy(step, j).start()
+    for copy in small:
+        copy.start()
+    pl.semaphore_wait(barrier, len(others))
+
+    home = t // 2
+    slot = lax.rem(t, 2)
+
+    def f_push(dt):
+        return pltpu.make_async_remote_copy(
+            src_ref=feat,
+            dst_ref=f.at[slot, s],
+            send_sem=f_send.at[dt],
+            recv_sem=f_recv.at[slot, s],
+            device_id={"seq": home, "tensor": lax.rem(t + dt, 4)},
+            device_id_type=MESH,
+        )
+
+    def f_pushes():
+        for dt in (2, 1, 3):
+            @pl.when(f_goes(dt))
+            def _(dt=dt):
+                f_push(dt).start()
+
+    def f_goes(dt):
+        if dt == 2:
+            return t < 4
+        return (t != 0) if dt == 3 else (t != 3)
+
+    @pl.when(home == s)
+    def _():
+        pltpu.make_async_copy(feat, f.at[slot, s], f_recv.at[slot, s]).start()
+
+    @pl.when(home != s)
+    def _():
+        f_push(0).start()
+
+    @pl.when(s == 0)
+    def _():
+        f_pushes()
+
+    relays = jnp.where(s == 0, t == 2, t == 1)
+
+    def f_relay(h):
+        far = 1 - near
+        return pltpu.make_async_remote_copy(
+            src_ref=f.at[far, h],
+            dst_ref=f.at[far, h],
+            send_sem=fr_send.at[h],
+            recv_sem=f_recv.at[far, h],
+            device_id={"seq": s, "tensor": lax.rem(t + 1 + 2 * s, 4)},
+            device_id_type=MESH,
+        )
+
+    def p_push(h, ct, j):
+        return pltpu.make_async_remote_copy(
+            src_ref=psend.at[h, ct, j],
+            dst_ref=precv.at[h, ct, j],
+            send_sem=p_send.at[h, ct, j],
+            recv_sem=p_recv.at[h, ct, j],
+            device_id=device(1, 0),
+            device_id_type=MESH,
+        )
+
+    def in_projection(h):
+        for step in range(2):
+            r = near if step == 0 else 1 - near
+            part = f.at[r, h]
+            pltpu.make_async_copy(part, part, f_recv.at[r, h]).wait()
+            if step == 1:
+
+                @pl.when(relays)
+                def _():
+                    f_relay(h).start()
+
+                if h == 0:
+
+                    @pl.when(s == 1)
+                    def _():
+                        f_pushes()
+
+            if h == 0:
+                for j in range(3):
+                    w_copy(step, j).wait()
+            depth = pl.ds(pl.multiple_of(r * deep, deep), deep)
+            for side in range(2):
+                target = psend if side == 0 else own
+                base = ((1 - s) if side == 0 else s) * half
+
+                @pl.loop(0, 6)
+                def _(idx, target=target, base=base, side=side, step=step, r=r, depth=depth):
+                    ct, j = idx // 3, lax.rem(idx, 3)
+                    columns = pl.ds(pl.multiple_of(base + ct * tile, tile), tile)
+                    part = jnp.dot(
+                        f[r, h], w[j, depth, columns], preferred_element_type=jnp.float32
+                    )
+                    for gl in range(2):
+                        piece = part[:, gl * lanes : (gl + 1) * lanes]
+                        if step == 0:
+                            target[h, ct, j, gl] = piece
+                        else:
+                            target[h, ct, j, gl] += piece
+                    if step == 1 and side == 0:
+                        p_push(h, ct, j).start()
+
+    first = lax.broadcasted_iota(jnp.int32, (8, lanes), 0)
+
+    def later(value, by):
+        return jnp.where(first >= by, pltpu.roll(value, by, 0), 0.0)
+
+    def g_push(h, dt, ct):
+        columns = pl.ds(pl.multiple_of(ct * tile, tile), tile)
+        return pltpu.make_async_remote_copy(
+            src_ref=gsend.at[h, :, columns],
+            dst_ref=gath.at[me, :, columns],
+            send_sem=g_send.at[h, dt, ct],
+            recv_sem=g_recv.at[me, ct],
+            device_id={"seq": h, "tensor": lax.rem(t + dt, 4)},
+            device_id_type=MESH,
+        )
+
+    def g_goes(h, dt):
+        return (s != h) if dt == 0 else f_goes(dt)
+
+    def convolve(h, ct, gl):
+        group = ct * 2 + gl
+        columns = pl.ds(pl.multiple_of(group * lanes, lanes), lanes)
+
+        @pl.loop(0, span, unroll=4)
+        def _(i):
+            at = pl.ds(i, 8, stride=span)
+            for j in range(3):
+                value = own.at[h, ct, j, gl][at, :] + precv.at[h, ct, j, gl][at, :]
+                proj[j, rim + i] = value.astype(jnp.bfloat16).astype(jnp.float32)
+
+        for j in range(3):
+            for k in range(rim):
+                last = proj[j, span + k]
+                if h == 0:
+                    proj[j, k] = later(last, 1)
+                    rims[group, j, k] = pltpu.roll(last, 1, 0)
+                else:
+                    proj[j, k] = jnp.where(first >= 1, pltpu.roll(last, 1, 0), rims[group, j, k])
+
+        tap = [
+            [jnp.broadcast_to(taps[j, k : k + 1, columns], (8, lanes)) for k in range(taps_count)]
+            for j in range(3)
+        ]
+
+        @pl.loop(0, span, unroll=2)
+        def _(i):
+            short = []
+            for j in range(3):
+                total = tap[j][0] * proj[j, rim + i]
+                for k in range(1, taps_count):
+                    total = total + tap[j][k] * proj[j, rim + i - k]
+                short.append(total)
+            gate[i] = short[0]
+            prod[i] = short[1] * short[2]
+
+        rate = [jnp.broadcast_to(decay[m : m + 1, columns], (8, lanes)) for m in range(modes)]
+        fall = [jnp.exp(-v) for v in rate]
+
+        def gather_state(i, state):
+            x = prod[i]
+            return tuple(a * v + x for a, v in zip(fall, state))
+
+        zero = jnp.zeros((8, lanes), jnp.float32)
+        state = lax.fori_loop(0, span, gather_state, (zero,) * modes, unroll=4)
+        start = []
+        for m in range(modes):
+            jump = jnp.exp(-rate[m] * float(span))
+            value = pltpu.roll(state[m], 1, 0)
+            value = jnp.where(first >= 1, value, 0.0 if h == 0 else carry[group, m])
+            for by in (1, 2, 4):
+                value = value + jump * later(value, by)
+                jump = jump * jump
+            start.append(value)
+        scale = [
+            jnp.broadcast_to(resid[m : m + 1, columns], (8, lanes)) * jnp.sqrt(2.0 * rate[m])
+            for m in range(modes)
+        ]
+        direct = jnp.broadcast_to(skip[:, columns], (8, lanes))
+
+        def emit(i, state):
+            x = prod[i]
+            state = tuple(a * v + x for a, v in zip(fall, state))
+            terms = [a * v for a, v in zip(scale, state)]
+            while len(terms) > 1:
+                terms = [a + b for a, b in zip(terms[::2], terms[1::2])]
+            gbuf[pl.ds(i, 8, stride=span), :] = gate[i] * (terms[0] + direct * x)
+            return state
+
+        state = lax.fori_loop(0, span, emit, tuple(start), unroll=2)
+        if h == 0:
+            for m in range(modes):
+                carry[group, m] = pltpu.roll(state[m], 1, 0)
+        gsend[h, :, columns] = gbuf[...].astype(jnp.bfloat16)
+
+    for h in range(2):
+        in_projection(h)
+        if h == 0:
+            for k in range(4):
+                ow_copy(k).start()
+            for copy in small:
+                copy.wait()
+
+        @pl.loop(0, 2)
+        def _(ct, h=h):
+            for j in range(3):
+                part = precv.at[h, ct, j]
+                pltpu.make_async_copy(part, part, p_recv.at[h, ct, j]).wait()
+
+            @pl.loop(0, 2)
+            def _(gl):
+                convolve(h, ct, gl)
+
+            for dt in (2, 1, 3, 0):
+
+                @pl.when(g_goes(h, dt))
+                def _(dt=dt):
+                    g_push(h, dt, ct).start()
+
+        @pl.when(s == h)
+        def _(h=h):
+            gath[me] = gsend[h]
+
+    for k in range(4):
+        ow_copy(k).wait()
+
+    middle = jnp.where(t == 1, True, t == 2)
+
+    def g_relay(source, ds, ct):
+        part = gath.at[source, :, pl.ds(ct * tile, tile)]
+        return pltpu.make_async_remote_copy(
+            src_ref=part,
+            dst_ref=part,
+            send_sem=gr_send.at[ds, ct],
+            recv_sem=g_recv.at[source, ct],
+            device_id={"seq": s, "tensor": jnp.where(t == 1, 0, 3)},
+            device_id_type=MESH,
+        )
+
+    for step in range(4):
+        z = arrival_order(t, step)
+        for ds in range(2):
+            source = z * 2 + lax.rem(s + ds, 2)
+            if (step, ds) != (0, 0):
+                for ct in range(2):
+                    part = gath.at[source, :, pl.ds(ct * tile, tile)]
+                    pltpu.make_async_copy(part, part, g_recv.at[source, ct]).wait()
+                    if step == 1:
+
+                        @pl.when(middle)
+                        def _(source=source, ds=ds, ct=ct):
+                            g_relay(source, ds, ct).start()
+
+            depth = pl.ds(pl.multiple_of(source * half, half), half)
+            part = jnp.dot(gath[source], ow[depth, :], preferred_element_type=jnp.float32)
+            if (step, ds) == (0, 0):
+                acc[...] = part
+            elif (step, ds) == (3, 1):
+                out[...] = (acc[...] + part).astype(out.dtype)
+            else:
+                acc[...] += part
+
+    for dt in (1, 2, 3):
+
+        @pl.when(f_goes(dt))
+        def _(dt=dt):
+            f_push(dt).wait_send()
+
+    @pl.when(home != s)
+    def _():
+        f_push(0).wait_send()
+
+    @pl.when(relays)
+    def _():
+        for h in range(2):
+            f_relay(h).wait_send()
+
+    @pl.when(middle)
+    def _():
+        for ds in range(2):
+            for ct in range(2):
+                g_relay(arrival_order(t, 1) * 2 + lax.rem(s + ds, 2), ds, ct).wait_send()
+
+    for h in range(2):
+        for ct in range(2):
+            for j in range(3):
+                p_push(h, ct, j).wait_send()
+            for dt in range(4):
+
+                @pl.when(g_goes(h, dt))
+                def _(h=h, ct=ct, dt=dt):
+                    g_push(h, dt, ct).wait_send()
+
+
+def fused_body(features, in_weight, short_taps, decay_rates, residues, skip_gain, out_weight):
+    rows, deep = features.shape
+    channels = in_weight.shape[2]
+    half = channels // 2
+    lanes = half // 4
+    span = rows // 8
+    modes = decay_rates.shape[0]
+    taps_count = short_taps.shape[1]
+    rim = taps_count - 1
+    f32, bf16 = jnp.float32, jnp.bfloat16
+    dma = pltpu.SemaphoreType.DMA
+    vmem = pl.BlockSpec(memory_space=pltpu.VMEM)
+    hbm = pl.BlockSpec(memory_space=pltpu.HBM)
+    sums = pltpu.VMEM((2, 2, 3, 2, rows, lanes), f32)
+    return pl.pallas_call(
+        fused_kernel,
+        out_shape=jax.ShapeDtypeStruct((rows, channels), bf16),
+        in_specs=[hbm] * 7,
+        out_specs=vmem,
+        scratch_shapes=[
+            pltpu.VMEM((2, 2, rows, deep), bf16),
+            pltpu.VMEM((3, 2 * deep, channels), bf16),
+            pltpu.VMEM((4 * channels, channels), bf16),
+            pltpu.VMEM((3, taps_count, half), f32),
+            pltpu.VMEM((modes, half), f32),
+            pltpu.VMEM((modes, half), f32),
+            pltpu.VMEM((1, half), f32),
+            sums,
+            sums,
+            sums,
+            pltpu.VMEM((3, span + rim, 8, lanes), f32),
+            pltpu.VMEM((span, 8, lanes), f32),
+            pltpu.VMEM((span, 8, lanes), f32),
+            pltpu.VMEM((4, 3, rim, 8, lanes), f32),
+            pltpu.VMEM((4, modes, 8, lanes), f32),
+            pltpu.VMEM((rows, lanes), f32),
+            pltpu.VMEM((2, rows, half), bf16),
+            pltpu.VMEM((8, rows, half), bf16),
+            pltpu.VMEM((rows, channels), f32),
+            dma((4,)),
+            dma((2, 2)),
+            dma((2,)),
+            dma((2, 3)),
+            dma((4,)),
+            dma((4,)),
+            dma((2, 2, 3)),
+            dma((2, 2, 3)),
+            dma((2, 4, 2)),
+            dma((8, 2)),
+            dma((2, 2)),
+        ],
+        compiler_params=pltpu.CompilerParams(
+            collective_id=0, has_side_effects=True, vmem_limit_bytes=50 * 1024 * 1024
+        ),
+        cost_estimate=pl.CostEstimate(
+            flops=2 * rows * 4 * channels * 4 * channels,
+            bytes_accessed=10 * deep * channels * 2,
+            transcendentals=0,
+        ),
+        name="mixer",
+    )(
+        features,
+        jnp.transpose(in_weight, (1, 0, 2)),
+        short_taps,
+        decay_rates,
+        residues,
+        skip_gain[None, :],
+        out_weight,
+    )
+
+
 def solution(mesh):
     in_specs = (
         P(("dp", "seq"), "tensor"),
@@ -105,4 +534,8 @@
         P(None, "tensor"),
     )
     out_specs = P(("dp", "seq"), "tensor")
+    if mesh.shape["seq"] == 2 and mesh.shape["tensor"] == 4:
+        return jax.shard_map(
+            fused_body, mesh=mesh, in_specs=in_specs, out_specs=out_specs, check_vma=False
+        )
     return jax.shard_map(body, mesh=mesh, in_specs=in_specs, out_specs=out_specs, check_vma=False)

time: 278 us -> 61.5 us (0.22)
  matrix products: 119 us -> 0 us
  waiting for transfers between devices: 61.3 us -> 0 us
  Pallas kernels: 0 us -> 56.2 us
  local copies, waits for them, and re-layouts: 57 us -> 4.91 us
  other arithmetic: 19.5 us -> 0 us
  between operations: 13.4 us -> 0.01 us
  blocking collectives: 4.69 us -> 0 us
    dot_general x6 -> x0, matrix products: 119 us -> none  [the longest x1 56.5 us: body(): inner = jnp.einsum('tsc,bsc->btc', toeplitz, pieces, precision=precise)]
    all_gather x3 -> x0, waiting for transfers between devices: 60.6 us -> none  [the longest x1 31.8 us: body(): piece = lax.all_gather(in_weight, 'seq', axis=0, tiled=True)]
    pallas_call x0 -> x1, Pallas kernels: none -> 56.2 us  [fused_body(): pl.pallas_call(fused_kernel, out_shape=jax.ShapeDtypeStruct((rows, channe...]
    dot_general x1 -> x0, local copies, waits for them, and re-layouts: 30.5 us -> none  [body(): toeplitz = jnp.einsum('tsk,kc->tsc', select, kernel, precision=precise)]
    unnamed x20 -> x11, local copies, waits for them, and re-layouts: 18 us -> 4.91 us
    unnamed x1 -> x0, other arithmetic: 11.8 us -> none
    add x4 -> x0, other arithmetic: 6.13 us -> none  [the longest x1 6.06 us: body(): short + short_taps[:, offset_lag, :][None] * extended[rim_rows - offset_l...]
    all_gather x2 -> x0, blocking collectives: 4.69 us -> none  [prefix_2(): gathered = jax.tree.map(lambda a: lax.all_gather(a, axis), part)]
  transfers between devices with their start and end apart: 4 -> 0, of which waited for: 2 -> 0; matrix products, arithmetic and copies ran while one was open for 26% -> 0% of each run, Pallas kernels for 0% -> 0%
where the time goes in v2:
time: 61.5 us; the launch traced here: 61.1 us
  Pallas kernels  56.2 us (91%)
  local copies, waits for them, and re-layouts  4.91 us (8%)
    pallas_call x1, Pallas kernels, fused_body(): pl.pallas_call(fused_kernel, out_shape=jax.ShapeDtypeStruct((rows, channe...  56.2 us
    unnamed x11, local copies, waits for them, and re-layouts  4.91 us

profile of v2, /device:TPU:1, one launch (start us, length us, event | category | flops | bytes accessed | tf_op | source)
XLA Modules:
  0.0 61.1 jit_solution(16708867856244759537)
XLA Ops:
  0.0 0.0 copy-start
  0.0 0.9 %copy-done = bf16[128,1024]{1,0:T(8,128)(2,1)S(1)} copy-done((bf16[128,1024]{1,0:T(8,128)(2,1)S(1)}, bf16[128,1024]{1,0:T(8,128)(2,1)}, u32[]{:S(2)}) %copy-start) | copy-done | bytes 262168
  1.0 0.0 copy-start.1
  1.0 0.9 %copy-done.1 = f32[3,7,1024]{2,1,0:T(8,128)S(1)} copy-done((f32[3,7,1024]{2,1,0:T(8,128)S(1)}, f32[3,7,1024]{2,1,0:T(8,128)}, u32[]{:S(2)}) %copy-start.1) | copy-done | bytes 86040
  1.8 0.0 copy-start.2
  1.8 0.8 %copy-done.2 = f32[16,1024]{1,0:T(8,128)S(1)} copy-done((f32[16,1024]{1,0:T(8,128)S(1)}, f32[16,1024]{1,0:T(8,128)}, u32[]{:S(2)}) %copy-start.2) | copy-done | bytes 65560
  2.7 0.0 copy-start.3
  2.7 0.8 %copy-done.3 = f32[16,1024]{1,0:T(8,128)S(1)} copy-done((f32[16,1024]{1,0:T(8,128)S(1)}, f32[16,1024]{1,0:T(8,128)}, u32[]{:S(2)}) %copy-start.3) | copy-done | bytes 65560
  3.5 0.0 copy-start.4
  3.5 0.7 %copy-done.4 = f32[1024]{0:T(1024)S(1)} copy-done((f32[1024]{0:T(1024)S(1)}, f32[1024]{0:T(1024)}, u32[]{:S(2)}) %copy-start.4) | copy-done | bytes 4120
  4.2 56.2 %mixer.1 = bf16[128,1024]{1,0:T(8,128)(2,1)S(1)} custom-call(bf16[128,1024]{1,0:T(8,128)(2,1)S(1)} %copy-done, bf16[3,2048,1024]{2,1,0:T(8,128)(2,1)} %bitcast.3, f32[3,7,1024]{2,1,0:T(8,128)S(1)} %copy-done.1, f32[16,1024]{1,0:T(8,128)S(1)} %copy-done.2, f32[16,1024]{1,0:T(8,128)S(1)} %copy-done.3, f32[1,1024]{1,0:T(1,128)S(1)} %bitcast.2, ...), custom_call_target="tpu_custom_call" | custom-call | flops 4294967296 | bytes 20971520 | tf_op jit(solution)/shard_map/mixer/pallas_call | solution.py:469
  60.4 0.7 %copy.9 = bf16[128,1024]{1,0:T(8,128)(2,1)} copy(bf16[128,1024]{1,0:T(8,128)(2,1)S(1)} %mixer.1) | data formatting | bytes 524288
Async XLA Ops:
  0.0 0.9 %copy-start = (bf16[128,1024]{1,0:T(8,128)(2,1)S(1)}, bf16[128,1024]{1,0:T(8,128)(2,1)}, u32[]{:S(2)}) copy-start(bf16[128,1024]{1,0:T(8,128)(2,1)} %feat.1) | copy-start | bytes 786436
  1.0 0.9 %copy-start.1 = (f32[3,7,1024]{2,1,0:T(8,128)S(1)}, f32[3,7,1024]{2,1,0:T(8,128)}, u32[]{:S(2)}) copy-start(f32[3,7,1024]{2,1,0:T(8,128)} %taps_hbm.1) | copy-start | bytes 258052
  1.8 0.8 %copy-start.2 = (f32[16,1024]{1,0:T(8,128)S(1)}, f32[16,1024]{1,0:T(8,128)}, u32[]{:S(2)}) copy-start(f32[16,1024]{1,0:T(8,128)} %decay_hbm.1) | copy-start | bytes 196612
  2.7 0.8 %copy-start.3 = (f32[16,1024]{1,0:T(8,128)S(1)}, f32[16,1024]{1,0:T(8,128)}, u32[]{:S(2)}) copy-start(f32[16,1024]{1,0:T(8,128)} %resid_hbm.1) | copy-start | bytes 196612
  3.5 0.7 %copy-start.4 = (f32[1024]{0:T(1024)S(1)}, f32[1024]{0:T(1024)}, u32[]{:S(2)}) copy-start(f32[1024]{0:T(1024)} %param.12) | copy-start | bytes 12292

commit v3 on v2

--- a/solution.py
+++ b/solution.py
@@ -110,11 +110,11 @@
 
 def fused_kernel(
     feat, w_hbm, taps_hbm, decay_hbm, resid_hbm, skip_hbm, ow_hbm, out,
-    f, w, ow, taps, decay, resid, skip, psend, precv, own, proj, prod, gate, rims, carry,
-    gbuf, gsend, gath, acc,
+    f, w, ow, taps, decay, resid, skip, plain, mixed_rows, tabs, psend, precv, own, proj, prod, gate,
+    rims, carry, gbuf, gsend, gath, acc,
     f_send, f_recv, fr_send, w_sem, ow_sem, c_sem, p_send, p_recv, g_send, g_recv, gr_send,
 ):
-    rows, deep = feat.shape
+    rows, deep = plain.shape
     lanes = own.shape[-1]
     half = lanes * 4
     tile = half // 2
@@ -148,6 +148,8 @@
         pltpu.make_async_copy(resid_hbm.at[:, mine], resid, c_sem.at[2]),
         pltpu.make_async_copy(skip_hbm.at[:, mine], skip, c_sem.at[3]),
     ]
+    load = pltpu.make_async_copy(feat, plain, c_sem.at[4])
+    load.start()
 
     barrier = pltpu.get_barrier_semaphore()
     for ds, dt in others:
@@ -157,6 +159,15 @@
             w_copy(step, j).start()
     for copy in small:
         copy.start()
+    down = lax.broadcasted_iota(jnp.int32, (rows, rows), 0)
+    across = lax.broadcasted_iota(jnp.int32, (rows, rows), 1)
+    to_steps = jnp.where(across == lax.rem(down, 8) * span + lax.div(down, 8), 1.0, 0.0)
+    to_tokens = jnp.where(down == lax.rem(across, 8) * span + lax.div(across, 8), 1.0, 0.0)
+    to_steps, to_tokens = to_steps.astype(jnp.bfloat16), to_tokens.astype(jnp.bfloat16)
+    load.wait()
+    mixed_rows[...] = jnp.dot(
+        to_steps, plain[...], preferred_element_type=jnp.float32
+    ).astype(jnp.bfloat16)
     pl.semaphore_wait(barrier, len(others))
 
     home = t // 2
@@ -164,7 +175,7 @@
 
     def f_push(dt):
         return pltpu.make_async_remote_copy(
-            src_ref=feat,
+            src_ref=mixed_rows,
             dst_ref=f.at[slot, s],
             send_sem=f_send.at[dt],
             recv_sem=f_recv.at[slot, s],
@@ -185,7 +196,7 @@
 
     @pl.when(home == s)
     def _():
-        pltpu.make_async_copy(feat, f.at[slot, s], f_recv.at[slot, s]).start()
+        pltpu.make_async_copy(mixed_rows, f.at[slot, s], f_recv.at[slot, s]).start()
 
     @pl.when(home != s)
     def _():
@@ -281,85 +292,77 @@
     def convolve(h, ct, gl):
         group = ct * 2 + gl
         columns = pl.ds(pl.multiple_of(group * lanes, lanes), lanes)
-
-        @pl.loop(0, span, unroll=4)
-        def _(i):
-            at = pl.ds(i, 8, stride=span)
-            for j in range(3):
-                value = own.at[h, ct, j, gl][at, :] + precv.at[h, ct, j, gl][at, :]
-                proj[j, rim + i] = value.astype(jnp.bfloat16).astype(jnp.float32)
-
+        short = []
         for j in range(3):
+            value = own[h, ct, j, gl] + precv[h, ct, j, gl]
+            proj[j, rim * 8 :] = value.astype(jnp.bfloat16).astype(jnp.float32)
             for k in range(rim):
-                last = proj[j, span + k]
+                last = pltpu.roll(proj[j, (span + k) * 8 : (span + k + 1) * 8], 1, 0)
                 if h == 0:
-                    proj[j, k] = later(last, 1)
-                    rims[group, j, k] = pltpu.roll(last, 1, 0)
+                    rims[group, j, k] = last
+                    last = jnp.where(first >= 1, last, 0.0)
                 else:
-                    proj[j, k] = jnp.where(first >= 1, pltpu.roll(last, 1, 0), rims[group, j, k])
-
-        tap = [
-            [jnp.broadcast_to(taps[j, k : k + 1, columns], (8, lanes)) for k in range(taps_count)]
-            for j in range(3)
-        ]
-
-        @pl.loop(0, span, unroll=2)
-        def _(i):
-            short = []
-            for j in range(3):
-                total = tap[j][0] * proj[j, rim + i]
-                for k in range(1, taps_count):
-                    total = total + tap[j][k] * proj[j, rim + i - k]
-                short.append(total)
-            gate[i] = short[0]
-            prod[i] = short[1] * short[2]
-
-        rate = [jnp.broadcast_to(decay[m : m + 1, columns], (8, lanes)) for m in range(modes)]
-        fall = [jnp.exp(-v) for v in rate]
-
-        def gather_state(i, state):
-            x = prod[i]
-            return tuple(a * v + x for a, v in zip(fall, state))
-
-        zero = jnp.zeros((8, lanes), jnp.float32)
-        state = lax.fori_loop(0, span, gather_state, (zero,) * modes, unroll=4)
-        start = []
-        for m in range(modes):
-            jump = jnp.exp(-rate[m] * float(span))
-            value = pltpu.roll(state[m], 1, 0)
-            value = jnp.where(first >= 1, value, 0.0 if h == 0 else carry[group, m])
-            for by in (1, 2, 4):
-                value = value + jump * later(value, by)
-                jump = jump * jump
-            start.append(value)
-        scale = [
-            jnp.broadcast_to(resid[m : m + 1, columns], (8, lanes)) * jnp.sqrt(2.0 * rate[m])
-            for m in range(modes)
-        ]
-        direct = jnp.broadcast_to(skip[:, columns], (8, lanes))
-
-        def emit(i, state):
-            x = prod[i]
-            state = tuple(a * v + x for a, v in zip(fall, state))
-            terms = [a * v for a, v in zip(scale, state)]
-            while len(terms) > 1:
-                terms = [a + b for a, b in zip(terms[::2], terms[1::2])]
-            gbuf[pl.ds(i, 8, stride=span), :] = gate[i] * (terms[0] + direct * x)
-            return state
-
-        state = lax.fori_loop(0, span, emit, tuple(start), unroll=2)
-        if h == 0:
-            for m in range(modes):
-                carry[group, m] = pltpu.roll(state[m], 1, 0)
-        gsend[h, :, columns] = gbuf[...].astype(jnp.bfloat16)
+                    last = jnp.where(first >= 1, last, rims[group, j, k])
+                proj[j, k * 8 : (k + 1) * 8] = last
+            total = taps[j, 0:1, columns] * proj[j, rim * 8 :]
+            for k in range(1, taps_count):
+                total = total + taps[j, k : k + 1, columns] * proj[j, pl.ds((rim - k) * 8, rows)]
+            short.append(total)
+        gate[...] = short[0]
+        prod[...] = short[1] * short[2]
+
+        def row(q, m):
+            return jnp.broadcast_to(tabs[q, m : m + 1, columns], (8, lanes))
+
+        def step_at(i):
+            return slice(i * 8, (i + 1) * 8)
+
+        size = modes // 2
+        for low in (0, size):
+            few = range(low, low + size)
+            fall = [row(0, m) for m in few]
+            state = [prod[step_at(0)]] * size
+            for i in range(1, span):
+                x = prod[step_at(i)]
+                state = [a * v + x for a, v in zip(fall, state)]
+            start = []
+            for m, v in zip(few, state):
+                value = pltpu.roll(v, 1, 0)
+                value = jnp.where(first >= 1, value, 0.0 if h == 0 else carry[group, m])
+                for q, by in enumerate((1, 2, 4)):
+                    value = value + row(1 + q, m) * later(value, by)
+                start.append(value)
+            scale = [row(4, m) for m in few]
+            state = start
+            for i in range(span):
+                x = prod[step_at(i)]
+                state = [a * v + x for a, v in zip(fall, state)]
+                terms = [a * v for a, v in zip(scale, state)]
+                while len(terms) > 1:
+                    terms = [a + b for a, b in zip(terms[::2], terms[1::2])]
+                if low == 0:
+                    gbuf[step_at(i)] = terms[0]
+                else:
+                    gbuf[step_at(i)] += terms[0]
+            if h == 0:
+                for m, v in zip(few, state):
+                    carry[group, m] = pltpu.roll(v, 1, 0)
+        result = gate[...] * (gbuf[...] + skip[:, columns] * prod[...])
+        gsend[h, :, columns] = result.astype(jnp.bfloat16)
+
+    for copy in small:
+        copy.wait()
+    jump = jnp.exp(-decay[...] * float(span))
+    tabs[0] = jnp.exp(-decay[...])
+    tabs[1] = jump
+    tabs[2] = jump * jump
+    tabs[3] = (jump * jump) * (jump * jump)
+    tabs[4] = resid[...] * jnp.sqrt(2.0 * decay[...])
+    for k in range(4):
+        ow_copy(k).start()
 
     for h in range(2):
         in_projection(h)
-        if h == 0:
-            for k in range(4):
-                ow_copy(k).start()
-            for copy in small:
-                copy.wait()
 
         @pl.loop(0, 2)
         def _(ct, h=h):
@@ -416,7 +419,10 @@
             if (step, ds) == (0, 0):
                 acc[...] = part
             elif (step, ds) == (3, 1):
-                out[...] = (acc[...] + part).astype(out.dtype)
+                done = (acc[...] + part).astype(out.dtype)
+                out[...] = jnp.dot(
+                    to_tokens, done, preferred_element_type=jnp.float32
+                ).astype(out.dtype)
             else:
                 acc[...] += part
 
@@ -479,12 +485,15 @@
             pltpu.VMEM((modes, half), f32),
             pltpu.VMEM((modes, half), f32),
             pltpu.VMEM((1, half), f32),
+            pltpu.VMEM((rows, deep), bf16),
+            pltpu.VMEM((rows, deep), bf16),
+            pltpu.VMEM((5, modes, half), f32),
             sums,
             sums,
             sums,
-            pltpu.VMEM((3, span + rim, 8, lanes), f32),
-            pltpu.VMEM((span, 8, lanes), f32),
-            pltpu.VMEM((span, 8, lanes), f32),
+            pltpu.VMEM((3, rows + 8 * rim, lanes), f32),
+            pltpu.VMEM((rows, lanes), f32),
+            pltpu.VMEM((rows, lanes), f32),
             pltpu.VMEM((4, 3, rim, 8, lanes), f32),
             pltpu.VMEM((4, modes, 8, lanes), f32),
             pltpu.VMEM((rows, lanes), f32),
@@ -496,7 +505,7 @@
             dma((2,)),
             dma((2, 3)),
             dma((4,)),
-            dma((4,)),
+            dma((5,)),
             dma((2, 2, 3)),
             dma((2, 2, 3)),
             dma((2, 4, 2)),
@@ -504,7 +513,7 @@
             dma((2, 2)),
         ],
         compiler_params=pltpu.CompilerParams(
-            collective_id=0, has_side_effects=True, vmem_limit_bytes=50 * 1024 * 1024
+            collective_id=0, has_side_effects=True, vmem_limit_bytes=60 * 1024 * 1024
         ),
         cost_estimate=pl.CostEstimate(
             flops=2 * rows * 4 * channels * 4 * channels,

time: 61.5 us -> 59 us (0.959)
  local copies, waits for them, and re-layouts: 4.91 us -> 1.67 us
  Pallas kernels: 56.2 us -> 57.1 us
    unnamed x11 -> x1, local copies, waits for them, and re-layouts: 4.91 us -> 1.67 us
    pallas_call x1, Pallas kernels: 56.2 us -> 57.1 us  [fused_body(): pl.pallas_call(fused_kernel, out_shape=jax.ShapeDtypeStruct((rows, channe...]
where the time goes in v3:
time: 59 us; the launch traced here: 58.8 us
  Pallas kernels  57.1 us (97%)
  local copies, waits for them, and re-layouts  1.67 us (3%)
    pallas_call x1, Pallas kernels, fused_body(): pl.pallas_call(fused_kernel, out_shape=jax.ShapeDtypeStruct((rows, channe...  57.1 us
    unnamed x1, local copies, waits for them, and re-layouts  1.67 us

profile of v3, /device:TPU:1, one launch (start us, length us, event | category | flops | bytes accessed | tf_op | source)
XLA Modules:
  0.0 58.8 jit_solution(6598671534068543069)
XLA Ops:
  0.0 57.1 %mixer.1 = bf16[128,1024]{1,0:T(8,128)(2,1)} custom-call(bf16[128,1024]{1,0:T(8,128)(2,1)} %feat.1, bf16[3,2048,1024]{2,1,0:T(8,128)(2,1)} %bitcast.2, f32[3,7,1024]{2,1,0:T(8,128)} %taps_hbm.1, f32[16,1024]{1,0:T(8,128)} %decay_hbm.1, f32[16,1024]{1,0:T(8,128)} %resid_hbm.1, f32[1,1024]{1,0:T(1,128)} %bitcast.3, bf16[4096,1024]{1,0:T(8,128)(2,1)} %ow_hbm.1), custom_call_target="tpu_custom_call" | custom-call | flops 4294967296 | bytes 20971520 | tf_op jit(solution)/shard_map/mixer/pallas_call | solution.py:475
  57.1 1.7 %copy.9 = bf16[128,1024]{1,0:T(8,128)(2,1)} copy(bf16[128,1024]{1,0:T(8,128)(2,1)} %mixer.1) | data formatting | bytes 524288

commit v4 on v3

--- a/solution.py
+++ b/solution.py
@@ -172,27 +172,18 @@
 
     home = t // 2
     slot = lax.rem(t, 2)
-
-    def f_push(dt):
+    along = jnp.where(s == 0, t, 3 - t)
+    ahead = jnp.where(s == 0, 1, 3)
+
+    def f_home():
         return pltpu.make_async_remote_copy(
             src_ref=mixed_rows,
             dst_ref=f.at[slot, s],
-            send_sem=f_send.at[dt],
+            send_sem=f_send,
             recv_sem=f_recv.at[slot, s],
-            device_id={"seq": home, "tensor": lax.rem(t + dt, 4)},
+            device_id=device(1, 0),
             device_id_type=MESH,
         )
-
-    def f_pushes():
-        for dt in (2, 1, 3):
-            @pl.when(f_goes(dt))
-            def _(dt=dt):
-                f_push(dt).start()
-
-    def f_goes(dt):
-        if dt == 2:
-            return t < 4
-        return (t != 0) if dt == 3 else (t != 3)
 
     @pl.when(home == s)
     def _():
@@ -200,24 +191,33 @@
 
     @pl.when(home != s)
     def _():
-        f_push(0).start()
-
-    @pl.when(s == 0)
-    def _():
-        f_pushes()
-
-    relays = jnp.where(s == 0, t == 2, t == 1)
-
-    def f_relay(h):
-        far = 1 - near
+        f_home().start()
+
+    def f_pass(h, step, back):
+        r = near if step == 0 else 1 - near
         return pltpu.make_async_remote_copy(
-            src_ref=f.at[far, h],
-            dst_ref=f.at[far, h],
-            send_sem=fr_send.at[h],
-            recv_sem=f_recv.at[far, h],
-            device_id={"seq": s, "tensor": lax.rem(t + 1 + 2 * s, 4)},
+            src_ref=f.at[r, h],
+            dst_ref=f.at[r, h],
+            send_sem=fr_send.at[h, step, back],
+            recv_sem=f_recv.at[r, h],
+            device_id={"seq": s, "tensor": lax.rem(t + (4 - ahead if back else ahead), 4)},
             device_id_type=MESH,
         )
+
+    def f_passes(step, back):
+        if step == 0:
+            return along == 1 if back else along < 3
+        return jnp.where(along == 1, True, along == 2)
+
+    def f_take(h, step):
+        r = near if step == 0 else 1 - near
+        part = f.at[r, h]
+        pltpu.make_async_copy(part, part, f_recv.at[r, h]).wait()
+        for back in range(2 - step):
+
+            @pl.when(f_passes(step, back))
+            def _(back=back):
+                f_pass(h, step, back).start()
 
     def p_push(h, ct, j):
         return pltpu.make_async_remote_copy(
@@ -232,43 +232,45 @@
     def in_projection(h):
         for step in range(2):
             r = near if step == 0 else 1 - near
-            part = f.at[r, h]
-            pltpu.make_async_copy(part, part, f_recv.at[r, h]).wait()
-            if step == 1:
-
-                @pl.when(relays)
-                def _():
-                    f_relay(h).start()
-
-                if h == 0:
-
-                    @pl.when(s == 1)
+            if h == 0:
+                f_take(0, step)
+                if step == 1:
+
+                    @pl.when(along < 2)
                     def _():
-                        f_pushes()
-
-            if h == 0:
+                        f_take(1, 0)
+
                 for j in range(3):
                     w_copy(step, j).wait()
+            elif step == 1:
+                f_take(1, 1)
             depth = pl.ds(pl.multiple_of(r * deep, deep), deep)
             for side in range(2):
                 target = psend if side == 0 else own
                 base = ((1 - s) if side == 0 else s) * half
 
-                @pl.loop(0, 6)
-                def _(idx, target=target, base=base, side=side, step=step, r=r, depth=depth):
-                    ct, j = idx // 3, lax.rem(idx, 3)
-                    columns = pl.ds(pl.multiple_of(base + ct * tile, tile), tile)
+                @pl.loop(0, 3)
+                def _(j, target=target, base=base, side=side, step=step, r=r, depth=depth):
+                    columns = pl.ds(pl.multiple_of(base, half), half)
                     part = jnp.dot(
                         f[r, h], w[j, depth, columns], preferred_element_type=jnp.float32
                     )
-                    for gl in range(2):
-                        piece = part[:, gl * lanes : (gl + 1) * lanes]
+                    for group in range(4):
+                        ct, gl = divmod(group, 2)
+                        piece = part[:, group * lanes : (group + 1) * lanes]
                         if step == 0:
                             target[h, ct, j, gl] = piece
                         else:
                             target[h, ct, j, gl] += piece
                     if step == 1 and side == 0:
-                        p_push(h, ct, j).start()
+                        for ct in range(2):
+                            p_push(h, ct, j).start()
+
+        if h == 0:
+
+            @pl.when(along > 1)
+            def _():
+                f_take(1, 0)
 
     first = lax.broadcasted_iota(jnp.int32, (8, lanes), 0)
 
@@ -287,7 +289,11 @@
         )
 
     def g_goes(h, dt):
-        return (s != h) if dt == 0 else f_goes(dt)
+        if dt == 0:
+            return s != h
+        if dt == 2:
+            return t < 4
+        return t < 4 if h == 0 else (t != 0) if dt == 3 else (t != 3)
 
     def convolve(h, ct, gl):
         group = ct * 2 + gl
@@ -387,7 +393,7 @@
     for k in range(4):
         ow_copy(k).wait()
 
-    middle = jnp.where(t == 1, True, t == 2)
+    middle = jnp.where(s == 0, False, jnp.where(t == 1, True, t == 2))
 
     def g_relay(source, ds, ct):
         part = gath.at[source, :, pl.ds(ct * tile, tile)]
@@ -426,20 +432,17 @@
             else:
                 acc[...] += part
 
-    for dt in (1, 2, 3):
-
-        @pl.when(f_goes(dt))
-        def _(dt=dt):
-            f_push(dt).wait_send()
-
     @pl.when(home != s)
     def _():
-        f_push(0).wait_send()
-
-    @pl.when(relays)
-    def _():
-        for h in range(2):
-            f_relay(h).wait_send()
+        f_home().wait_send()
+
+    for h in range(2):
+        for step in range(2):
+            for back in range(2 - step):
+
+                @pl.when(f_passes(step, back))
+                def _(h=h, step=step, back=back):
+                    f_pass(h, step, back).wait_send()
 
     @pl.when(middle)
     def _():
@@ -500,9 +503,9 @@
             pltpu.VMEM((2, rows, half), bf16),
             pltpu.VMEM((8, rows, half), bf16),
             pltpu.VMEM((rows, channels), f32),
-            dma((4,)),
+            dma,
             dma((2, 2)),
-            dma((2,)),
+            dma((2, 2, 2)),
             dma((2, 3)),
             dma((4,)),
             dma((5,)),

time: 59 us -> 60.3 us (1.022)
  Pallas kernels: 57.1 us -> 58.5 us
    pallas_call x1, Pallas kernels: 57.1 us -> 58.5 us  [fused_body(): pl.pallas_call(fused_kernel, out_shape=jax.ShapeDtypeStruct((rows, channe...]
where the time goes in v4:
time: 60.3 us; the launch traced here: 60.1 us
  Pallas kernels  58.5 us (97%)
  local copies, waits for them, and re-layouts  1.67 us (3%)
    pallas_call x1, Pallas kernels, fused_body(): pl.pallas_call(fused_kernel, out_shape=jax.ShapeDtypeStruct((rows, channe...  58.5 us
    unnamed x1, local copies, waits for them, and re-layouts  1.67 us

profile of v4, /device:TPU:1, one launch (start us, length us, event | category | flops | bytes accessed | tf_op | source)
XLA Modules:
  0.0 60.1 jit_solution(16917410636431640078)
XLA Ops:
  0.0 58.5 %mixer.1 = bf16[128,1024]{1,0:T(8,128)(2,1)} custom-call(bf16[128,1024]{1,0:T(8,128)(2,1)} %feat.1, bf16[3,2048,1024]{2,1,0:T(8,128)(2,1)} %bitcast.2, f32[3,7,1024]{2,1,0:T(8,128)} %taps_hbm.1, f32[16,1024]{1,0:T(8,128)} %decay_hbm.1, f32[16,1024]{1,0:T(8,128)} %resid_hbm.1, f32[1,1024]{1,0:T(1,128)} %bitcast.3, bf16[4096,1024]{1,0:T(8,128)(2,1)} %ow_hbm.1), custom_call_target="tpu_custom_call" | custom-call | flops 4294967296 | bytes 20971520 | tf_op jit(solution)/shard_map/mixer/pallas_call | solution.py:478
  58.5 1.7 %copy.9 = bf16[128,1024]{1,0:T(8,128)(2,1)} copy(bf16[128,1024]{1,0:T(8,128)(2,1)} %mixer.1) | data formatting | bytes 524288

commit v5 on v4

--- a/solution.py
+++ b/solution.py
@@ -100,14 +100,6 @@
     return mixed.astype(jnp.bfloat16)
 
 
-def arrival_order(place, step):
-    table = ((0, 1, 2, 3), (1, 3, 0, 2), (2, 0, 3, 1), (3, 2, 1, 0))
-    found = jnp.int32(table[0][step])
-    for at in range(1, 4):
-        found = jnp.where(place == at, jnp.int32(table[at][step]), found)
-    return found
-
-
 def fused_kernel(
     feat, w_hbm, taps_hbm, decay_hbm, resid_hbm, skip_hbm, ow_hbm, out,
     f, w, ow, taps, decay, resid, skip, plain, mixed_rows, tabs, psend, precv, own, proj, prod, gate,
@@ -242,8 +234,18 @@
 
                 for j in range(3):
                     w_copy(step, j).wait()
-            elif step == 1:
-                f_take(1, 1)
+            elif step == 0:
+
+                @pl.when(along == 3)
+                def _():
+                    f_take(1, 0)
+
+            else:
+
+                @pl.when(jnp.where(along == 0, True, along == 3))
+                def _():
+                    f_take(1, 1)
+
             depth = pl.ds(pl.multiple_of(r * deep, deep), deep)
             for side in range(2):
                 target = psend if side == 0 else own
@@ -268,9 +270,13 @@
 
         if h == 0:
 
-            @pl.when(along > 1)
+            @pl.when(along == 2)
             def _():
                 f_take(1, 0)
+
+            @pl.when(f_passes(1, 0))
+            def _():
+                f_take(1, 1)
 
     first = lax.broadcasted_iota(jnp.int32, (8, lanes), 0)
 
@@ -291,9 +297,9 @@
     def g_goes(h, dt):
         if dt == 0:
             return s != h
-        if dt == 2:
-            return t < 4
-        return t < 4 if h == 0 else (t != 0) if dt == 3 else (t != 3)
+        if h == 0 or dt == 2:
+            return t < 4 * (1 - h)
+        return (t != 0) if dt == 3 else (t != 3)
 
     def convolve(h, ct, gl):
         group = ct * 2 + gl
@@ -393,44 +399,66 @@
     for k in range(4):
         ow_copy(k).wait()
 
-    middle = jnp.where(s == 0, False, jnp.where(t == 1, True, t == 2))
-
-    def g_relay(source, ds, ct):
+    def g_pass(source, ct, back):
         part = gath.at[source, :, pl.ds(ct * tile, tile)]
         return pltpu.make_async_remote_copy(
             src_ref=part,
             dst_ref=part,
-            send_sem=gr_send.at[ds, ct],
+            send_sem=gr_send.at[source, ct],
             recv_sem=g_recv.at[source, ct],
-            device_id={"seq": s, "tensor": jnp.where(t == 1, 0, 3)},
+            device_id={"seq": s, "tensor": lax.rem(t + (3 if back else 1), 4)},
             device_id_type=MESH,
         )
 
-    for step in range(4):
-        z = arrival_order(t, step)
-        for ds in range(2):
-            source = z * 2 + lax.rem(s + ds, 2)
-            if (step, ds) != (0, 0):
-                for ct in range(2):
-                    part = gath.at[source, :, pl.ds(ct * tile, tile)]
-                    pltpu.make_async_copy(part, part, g_recv.at[source, ct]).wait()
-                    if step == 1:
-
-                        @pl.when(middle)
-                        def _(source=source, ds=ds, ct=ct):
-                            g_relay(source, ds, ct).start()
-
-            depth = pl.ds(pl.multiple_of(source * half, half), half)
-            part = jnp.dot(gath[source], ow[depth, :], preferred_element_type=jnp.float32)
-            if (step, ds) == (0, 0):
-                acc[...] = part
-            elif (step, ds) == (3, 1):
-                done = (acc[...] + part).astype(out.dtype)
-                out[...] = jnp.dot(
-                    to_tokens, done, preferred_element_type=jnp.float32
-                ).astype(out.dtype)
-            else:
-                acc[...] += part
+    def g_passes(back):
+        return jnp.where(s == 0, False, (t > 0) if back else (t < 3))
+
+    def add_from(source):
+        depth = pl.ds(pl.multiple_of(source * half, half), half)
+        acc[...] += jnp.dot(gath[source], ow[depth, :], preferred_element_type=jnp.float32)
+
+    def g_wait(source, ct):
+        part = gath.at[source, :, pl.ds(ct * tile, tile)]
+        pltpu.make_async_copy(part, part, g_recv.at[source, ct]).wait()
+
+    steps = [(away, back) for away in (1, 2, 3) for back in range(2)]
+
+    def has(away, back):
+        return t + away < 4 if back else t >= away
+
+    acc[...] = jnp.zeros_like(acc)
+    add_from(me)
+    for ct in range(2):
+        g_wait(t * 2 + 1 - s, ct)
+    add_from(t * 2 + 1 - s)
+    for away, back in steps:
+
+        @pl.when(has(away, back))
+        def _(away=away, back=back):
+            z = t + away if back else t - away
+            for ct in range(2):
+                for ds in range(2):
+                    g_wait(z * 2 + ds, ct)
+
+                    @pl.when(g_passes(back))
+                    def _(ct=ct, ds=ds):
+                        g_pass(z * 2 + ds, ct, back).start()
+
+            for ds in range(2):
+                add_from(z * 2 + ds)
+
+    out[...] = jnp.dot(
+        to_tokens, acc[...].astype(out.dtype), preferred_element_type=jnp.float32
+    ).astype(out.dtype)
+
+    for away, back in steps:
+
+        @pl.when(jnp.where(has(away, back), g_passes(back), False))
+        def _(away=away, back=back):
+            z = t + away if back else t - away
+            for ct in range(2):
+                for ds in range(2):
+                    g_pass(z * 2 + ds, ct, back).wait_send()
 
     @pl.when(home != s)
     def _():
@@ -443,12 +471,6 @@
                 @pl.when(f_passes(step, back))
                 def _(h=h, step=step, back=back):
                     f_pass(h, step, back).wait_send()
-
-    @pl.when(middle)
-    def _():
-        for ds in range(2):
-            for ct in range(2):
-                g_relay(arrival_order(t, 1) * 2 + lax.rem(s + ds, 2), ds, ct).wait_send()
 
     for h in range(2):
         for ct in range(2):
@@ -513,7 +535,7 @@
             dma((2, 2, 3)),
             dma((2, 4, 2)),
             dma((8, 2)),
-            dma((2, 2)),
+            dma((8, 2)),
         ],
         compiler_params=pltpu.CompilerParams(
             collective_id=0, has_side_effects=True, vmem_limit_bytes=60 * 1024 * 1024

time: 60.3 us -> 53.4 us (0.89)
  Pallas kernels: 58.5 us -> 51.5 us
    pallas_call x1, Pallas kernels: 58.5 us -> 51.5 us  [fused_body(): pl.pallas_call(fused_kernel, out_shape=jax.ShapeDtypeStruct((rows, channe...]
where the time goes in v5:
time: 53.4 us; the launch traced here: 53.2 us
  Pallas kernels  51.5 us (96%)
  local copies, waits for them, and re-layouts  1.67 us (3%)
    pallas_call x1, Pallas kernels, fused_body(): pl.pallas_call(fused_kernel, out_shape=jax.ShapeDtypeStruct((rows, channe...  51.5 us
    unnamed x1, local copies, waits for them, and re-layouts  1.67 us

profile of v5, /device:TPU:1, one launch (start us, length us, event | category | flops | bytes accessed | tf_op | source)
XLA Modules:
  0.0 53.2 jit_solution(5201422667048220849)
XLA Ops:
  0.0 51.5 %mixer.1 = bf16[128,1024]{1,0:T(8,128)(2,1)} custom-call(bf16[128,1024]{1,0:T(8,128)(2,1)} %feat.1, bf16[3,2048,1024]{2,1,0:T(8,128)(2,1)} %bitcast.2, f32[3,7,1024]{2,1,0:T(8,128)} %taps_hbm.1, f32[16,1024]{1,0:T(8,128)} %decay_hbm.1, f32[16,1024]{1,0:T(8,128)} %resid_hbm.1, f32[1,1024]{1,0:T(1,128)} %bitcast.3, bf16[4096,1024]{1,0:T(8,128)(2,1)} %ow_hbm.1), custom_call_target="tpu_custom_call" | custom-call | flops 4294967296 | bytes 20971520 | tf_op jit(solution)/shard_map/mixer/pallas_call | solution.py:500
  51.5 1.7 %copy.9 = bf16[128,1024]{1,0:T(8,128)(2,1)} copy(bf16[128,1024]{1,0:T(8,128)(2,1)} %mixer.1) | data formatting | bytes 524288

commit v6 on v5

--- a/solution.py
+++ b/solution.py
@@ -284,10 +284,9 @@
         return jnp.where(first >= by, pltpu.roll(value, by, 0), 0.0)
 
     def g_push(h, dt, ct):
-        columns = pl.ds(pl.multiple_of(ct * tile, tile), tile)
         return pltpu.make_async_remote_copy(
-            src_ref=gsend.at[h, :, columns],
-            dst_ref=gath.at[me, :, columns],
+            src_ref=gsend.at[h, ct],
+            dst_ref=gath.at[me, ct],
             send_sem=g_send.at[h, dt, ct],
             recv_sem=g_recv.at[me, ct],
             device_id={"seq": h, "tensor": lax.rem(t + dt, 4)},
@@ -360,7 +359,8 @@
                 for m, v in zip(few, state):
                     carry[group, m] = pltpu.roll(v, 1, 0)
         result = gate[...] * (gbuf[...] + skip[:, columns] * prod[...])
-        gsend[h, :, columns] = result.astype(jnp.bfloat16)
+        part = pl.ds(pl.multiple_of(gl * lanes, lanes), lanes)
+        gsend[h, ct, :, part] = result.astype(jnp.bfloat16)
 
     for copy in small:
         copy.wait()
@@ -400,42 +400,47 @@
         ow_copy(k).wait()
 
     def g_pass(source, ct, back):
-        part = gath.at[source, :, pl.ds(ct * tile, tile)]
+        part = gath.at[source, ct]
         return pltpu.make_async_remote_copy(
             src_ref=part,
             dst_ref=part,
             send_sem=gr_send.at[source, ct],
             recv_sem=g_recv.at[source, ct],
-            device_id={"seq": s, "tensor": lax.rem(t + (3 if back else 1), 4)},
+            device_id={"seq": s, "tensor": lax.rem(t + jnp.where(back == 1, 3, 1), 4)},
             device_id_type=MESH,
         )
 
     def g_passes(back):
-        return jnp.where(s == 0, False, (t > 0) if back else (t < 3))
+        return jnp.where(s == 0, False, jnp.where(back == 1, t > 0, t < 3))
 
     def add_from(source):
-        depth = pl.ds(pl.multiple_of(source * half, half), half)
-        acc[...] += jnp.dot(gath[source], ow[depth, :], preferred_element_type=jnp.float32)
+        total = acc[...]
+        for ct in range(2):
+            depth = pl.ds(pl.multiple_of(source * half + ct * tile, tile), tile)
+            total += jnp.dot(gath[source, ct], ow[depth, :], preferred_element_type=jnp.float32)
+        acc[...] = total
 
     def g_wait(source, ct):
-        part = gath.at[source, :, pl.ds(ct * tile, tile)]
+        part = gath.at[source, ct]
         pltpu.make_async_copy(part, part, g_recv.at[source, ct]).wait()
 
-    steps = [(away, back) for away in (1, 2, 3) for back in range(2)]
+    inner = jnp.where(t < 2, 1, 0)
+    steps = [(away, turn) for away in (1, 2, 3) for turn in range(2)]
 
     def has(away, back):
-        return t + away < 4 if back else t >= away
+        return jnp.where(back == 1, t + away < 4, t >= away)
 
     acc[...] = jnp.zeros_like(acc)
     add_from(me)
     for ct in range(2):
         g_wait(t * 2 + 1 - s, ct)
     add_from(t * 2 + 1 - s)
-    for away, back in steps:
+    for away, turn in steps:
+        back = inner if turn == 0 else 1 - inner
 
         @pl.when(has(away, back))
         def _(away=away, back=back):
-            z = t + away if back else t - away
+            z = jnp.where(back == 1, t + away, t - away)
             for ct in range(2):
                 for ds in range(2):
                     g_wait(z * 2 + ds, ct)
@@ -451,11 +456,12 @@
         to_tokens, acc[...].astype(out.dtype), preferred_element_type=jnp.float32
     ).astype(out.dtype)
 
-    for away, back in steps:
+    for away, turn in steps:
+        back = inner if turn == 0 else 1 - inner
 
         @pl.when(jnp.where(has(away, back), g_passes(back), False))
         def _(away=away, back=back):
-            z = t + away if back else t - away
+            z = jnp.where(back == 1, t + away, t - away)
             for ct in range(2):
                 for ds in range(2):
                     g_pass(z * 2 + ds, ct, back).wait_send()
@@ -522,8 +528,8 @@
             pltpu.VMEM((4, 3, rim, 8, lanes), f32),
             pltpu.VMEM((4, modes, 8, lanes), f32),
             pltpu.VMEM((rows, lanes), f32),
-            pltpu.VMEM((2, rows, half), bf16),
-            pltpu.VMEM((8, rows, half), bf16),
+            pltpu.VMEM((2, 2, rows, half // 2), bf16),
+            pltpu.VMEM((8, 2, rows, half // 2), bf16),
             pltpu.VMEM((rows, channels), f32),
             dma,
             dma((2, 2)),

time: 53.4 us -> 53.4 us (level)
  no operation moved by 1% of the time
where the time goes in v6:
time: 53.4 us; the launch traced here: 53.2 us
  Pallas kernels  51.5 us (96%)
  local copies, waits for them, and re-layouts  1.67 us (3%)
    pallas_call x1, Pallas kernels, fused_body(): pl.pallas_call(fused_kernel, out_shape=jax.ShapeDtypeStruct((rows, channe...  51.5 us
    unnamed x1, local copies, waits for them, and re-layouts  1.67 us

profile of v6, /device:TPU:1, one launch (start us, length us, event | category | flops | bytes accessed | tf_op | source)
XLA Modules:
  0.0 53.2 jit_solution(6557891971791119664)
XLA Ops:
  0.0 51.5 %mixer.1 = bf16[128,1024]{1,0:T(8,128)(2,1)} custom-call(bf16[128,1024]{1,0:T(8,128)(2,1)} %feat.1, bf16[3,2048,1024]{2,1,0:T(8,128)(2,1)} %bitcast.2, f32[3,7,1024]{2,1,0:T(8,128)} %taps_hbm.1, f32[16,1024]{1,0:T(8,128)} %decay_hbm.1, f32[16,1024]{1,0:T(8,128)} %resid_hbm.1, f32[1,1024]{1,0:T(1,128)} %bitcast.3, bf16[4096,1024]{1,0:T(8,128)(2,1)} %ow_hbm.1), custom_call_target="tpu_custom_call" | custom-call | flops 4294967296 | bytes 20971520 | tf_op jit(solution)/shard_map/mixer/pallas_call | solution.py:506
  51.5 1.7 %copy.9 = bf16[128,1024]{1,0:T(8,128)(2,1)} copy(bf16[128,1024]{1,0:T(8,128)(2,1)} %mixer.1) | data formatting | bytes 524288

commit v7 on v6

--- a/solution.py
+++ b/solution.py
@@ -373,8 +373,18 @@
     for k in range(4):
         ow_copy(k).start()
 
+    def g_start(h, ct):
+        for dt in (2, 1, 3, 0):
+
+            @pl.when(g_goes(h, dt))
+            def _(dt=dt):
+                g_push(h, dt, ct).start()
+
     for h in range(2):
         in_projection(h)
+        if h == 1:
+            for ct in range(2):
+                g_start(0, ct)
 
         @pl.loop(0, 2)
         def _(ct, h=h):
@@ -386,11 +396,8 @@
             def _(gl):
                 convolve(h, ct, gl)
 
-            for dt in (2, 1, 3, 0):
-
-                @pl.when(g_goes(h, dt))
-                def _(dt=dt):
-                    g_push(h, dt, ct).start()
+            if h == 1:
+                g_start(1, ct)
 
         @pl.when(s == h)
         def _(h=h):

time: 53.4 us -> 53.5 us (level)
  no operation moved by 1% of the time
where the time goes in v7:
time: 53.5 us; the launch traced here: 53.3 us
  Pallas kernels  51.7 us (97%)
  local copies, waits for them, and re-layouts  1.67 us (3%)
    pallas_call x1, Pallas kernels, fused_body(): pl.pallas_call(fused_kernel, out_shape=jax.ShapeDtypeStruct((rows, channe...  51.7 us
    unnamed x1, local copies, waits for them, and re-layouts  1.67 us

profile of v7, /device:TPU:1, one launch (start us, length us, event | category | flops | bytes accessed | tf_op | source)
XLA Modules:
  0.0 53.3 jit_solution(7857091457257298284)
XLA Ops:
  0.0 51.7 %mixer.1 = bf16[128,1024]{1,0:T(8,128)(2,1)} custom-call(bf16[128,1024]{1,0:T(8,128)(2,1)} %feat.1, bf16[3,2048,1024]{2,1,0:T(8,128)(2,1)} %bitcast.2, f32[3,7,1024]{2,1,0:T(8,128)} %taps_hbm.1, f32[16,1024]{1,0:T(8,128)} %decay_hbm.1, f32[16,1024]{1,0:T(8,128)} %resid_hbm.1, f32[1,1024]{1,0:T(1,128)} %bitcast.3, bf16[4096,1024]{1,0:T(8,128)(2,1)} %ow_hbm.1), custom_call_target="tpu_custom_call" | custom-call | flops 4294967296 | bytes 20971520 | tf_op jit(solution)/shard_map/mixer/pallas_call | solution.py:513
  51.7 1.7 %copy.9 = bf16[128,1024]{1,0:T(8,128)(2,1)} copy(bf16[128,1024]{1,0:T(8,128)(2,1)} %mixer.1) | data formatting | bytes 524288
